TPU v7x, 128 devices: a whole 4x4x4 slice. The times are simulated.
128 devices in a mesh: sec: 4 (over z_lo, core), gx: 8 (over x, z_hi), gy: 4 (over y).
Axes of the slice: x: 4, y: 4, z: 4 (z_hi: 2, z_lo: 2; z = z_hi * 2 + z_lo), core: 2. Of those that a mesh axis runs over, the one named last changes fastest.
Arguments:
- surface: float32 [64, 2, 256, 512], P(None, None, 'gx', 'gy'), may hold values from -6 to 6
- coef_table: float32 [64, 9, 2, 64], replicated, may hold values from -0.3 to 0.3
- vel_index: int32 [4, 256, 512], P('sec', 'gx', 'gy'), may hold values from 0 to 63
Outputs:
- image: float32 [4, 256, 512], P('sec', 'gx', 'gy')
All inputs are finite; a program needn't handle non-finite values.
Results may differ from a plain program's by a relative error of at most 0.0003.
Values sent between devices are 32-bit elements; how exact they have to be, the bound alone decides.
No kernel may reach another device: no remote copies, remote signals or barrier semaphores. Data moves between devices by JAX's collectives and lax.ppermute only.
A program may use at most 128 MiB of HBM per device.

v0:
```python
import jax
import jax.numpy as jnp
from jax import lax
from jax.sharding import PartitionSpec as P

DEP_SEC = 1


def extended(block, sides, width):
    for axis, dim in sides:
        count = lax.axis_size(axis)
        forward = [(i, i + 1) for i in range(count - 1)]
        backward = [(target, source) for source, target in forward]
        low = lax.ppermute(
            lax.slice_in_dim(block, block.shape[dim] - width, None, axis=dim), axis, forward
        )
        high = lax.ppermute(lax.slice_in_dim(block, 0, width, axis=dim), axis, backward)
        block = jnp.concatenate([low, block, high], axis=dim)
    return block


def shifted(array, axis, by):
    size = lax.axis_size(axis)
    pairs = [(i, i + by) for i in range(size) if 0 <= i + by < size]
    return lax.ppermute(array, axis, pairs)


def mclellan_local(padded):
    rows = padded[:, :, :-2, :] + 2.0 * padded[:, :, 1:-1, :] + padded[:, :, 2:, :]
    both = rows[:, :, :, :-2] + 2.0 * rows[:, :, :, 1:-1] + rows[:, :, :, 2:]
    return 0.125 * both - padded[:, :, 1:-1, 1:-1]


def complex_mul(coeff, field):
    real = coeff[:, 0] * field[:, 0] - coeff[:, 1] * field[:, 1]
    imag = coeff[:, 0] * field[:, 1] + coeff[:, 1] * field[:, 0]
    return jnp.stack([real, imag], axis=1)


def per_device(surface, coef_table, vel_index):
    freq_count = surface.shape[0]
    tile_rows = surface.shape[2]
    tile_cols = surface.shape[3]
    top_order = coef_table.shape[1] - 1
    table_size = coef_table.shape[3]
    sections = lax.axis_size("sec")
    section_id = lax.axis_index("sec")
    entries = jnp.arange(table_size, dtype=jnp.int32)

    def extrapolate(field, coeffs):

        def apply_op(value):
            padded = extended(value, (("gx", 2), ("gy", 3)), 1)
            return mclellan_local(padded)

        before = field
        current = apply_op(field)
        total = complex_mul(coeffs[:, 0], before) + complex_mul(coeffs[:, 1], current)
        for order in range(2, top_order + 1):
            following = 2.0 * apply_op(current) - before
            total = total + complex_mul(coeffs[:, order], following)
            before, current = (current, following)
        return total

    batch_size = 8
    batch_size = min(batch_size, freq_count)
    batches = freq_count // batch_size
    onehot = (vel_index.reshape(DEP_SEC, 1, -1) == entries[None, :, None]).astype(jnp.float32)

    def advance(tick, carry):
        plane, image = carry
        block = tick - section_id
        active = (block >= 0) & (block < batches)
        block_safe = jnp.clip(block, 0, batches - 1)
        fresh = lax.dynamic_slice_in_dim(
            surface, jnp.clip(tick, 0, batches - 1) * batch_size, batch_size, 0
        )
        plane = jnp.where(section_id == 0, fresh, plane)
        table = lax.dynamic_slice_in_dim(
            coef_table, block_safe * batch_size, batch_size, 0
        ).reshape(-1, table_size)
        coeffs = jnp.dot(table, onehot[0], precision=lax.Precision.HIGHEST)
        coeffs = coeffs.reshape(batch_size, top_order + 1, 2, tile_rows, tile_cols)
        plane = extrapolate(plane, coeffs)
        image = image.at[0].add(jnp.where(active, jnp.sum(plane[:, 0], axis=0), 0.0))
        sent = shifted(plane, "sec", 1)
        return (sent, image)

    plane_init = jnp.zeros((batch_size, 2, tile_rows, tile_cols), jnp.float32)
    image_init = jnp.zeros((DEP_SEC, tile_rows, tile_cols), jnp.float32)
    last_plane, image = lax.fori_loop(0, batches + sections - 1, advance, (plane_init, image_init))
    return image


def solution(mesh):
    in_specs = (P(None, None, "gx", "gy"), P(), P("sec", "gx", "gy"))
    out_specs = P("sec", "gx", "gy")
    return jax.shard_map(
        per_device, mesh=mesh, in_specs=in_specs, out_specs=out_specs, check_vma=False
    )
```

profile of v0, /device:TPU:62, one launch (start us, length us, event | category | flops | bytes accessed | tf_op | source)
XLA Modules:
  0.0 2096.7 jit_solution(16203805149140780341)
XLA Ops:
  0.0 2096.6 %while.20 = (s32[]{:T(128)}, f32[8,2,32,128]{3,2,1,0:T(8,128)S(1)}, f32[1,32,128]{2,1,0:T(8,128)}, s32[]{:T(128)}, f32[64,9,2,64]{3,2,1,0:T(2,128)}, /*index=5*/...) while((s32[]{:T(128)}, f32[8,2,32,128]{3,2,1,0:T(8,128)S(1)}, ...), condition=%wide.region_2.3_spmd.clone, body=%wide.region_0.2_spmd.clone.sunk | while | flops 465012736 | bytes 54539928 | solution.py:91
  8.4 5.7 collective-permute-done.1
  169.5 5.4 collective-permute-start.29
  199.9 5.4 collective-permute-start.1
  221.7 5.4 collective-permute-start.5
  243.4 5.4 collective-permute-start.9
  265.1 5.4 collective-permute-start.13
  311.6 5.4 collective-permute-start.21
  334.5 5.4 collective-permute-start.25
  345.6 6.4 collective-permute-done.26
  359.4 5.4 collective-permute-start.29
  389.9 5.4 collective-permute-start.1
  411.7 5.4 collective-permute-start.5
  433.4 5.4 collective-permute-start.9
  455.1 5.4 collective-permute-start.13
  501.6 5.4 collective-permute-start.21
  524.5 5.4 collective-permute-start.25
  535.6 6.4 collective-permute-done.26
  549.3 5.4 collective-permute-start.29
  579.9 5.4 collective-permute-start.1
  601.6 5.4 collective-permute-start.5
  623.4 5.4 collective-permute-start.9
  645.1 5.4 collective-permute-start.13
  691.6 5.4 collective-permute-start.21
  714.4 5.4 collective-permute-start.25
  725.6 6.4 collective-permute-done.26
  739.3 5.4 collective-permute-start.29
  769.8 5.4 collective-permute-start.1
  813.3 5.4 collective-permute-start.9
  835.0 5.4 collective-permute-start.13
  915.5 6.4 collective-permute-done.26
  929.2 5.4 collective-permute-start.29
  959.8 5.4 collective-permute-start.1
  981.5 5.4 collective-permute-start.5
  1071.5 5.4 collective-permute-start.21
  1105.5 6.4 collective-permute-done.26
  1261.5 5.4 collective-permute-start.21
  1295.5 6.4 collective-permute-done.26
  1485.4 6.4 collective-permute-done.26
  1499.1 5.4 collective-permute-start.29
  1551.4 5.4 collective-permute-start.5
  1573.2 5.4 collective-permute-start.9
  1594.9 5.4 collective-permute-start.13
  1641.4 5.4 collective-permute-start.21
  1675.4 6.4 collective-permute-done.26
  1865.4 6.4 collective-permute-done.26
  2044.2 5.4 collective-permute-start.25
  2055.3 6.4 collective-permute-done.26
  (1451 shorter events, 1823.4 us)
Async XLA Ops:
  17.1 9.6 collective-permute-start.3
  74.4 11.2 collective-permute-start.12
  157.2 9.6 collective-permute-start.27
  263.2 11.2 collective-permute-start.12
  265.1 9.2 collective-permute-start.13
  321.7 10.1 collective-permute-start.23
  342.6 9.4 collective-permute-start.26
  344.3 12.4 collective-permute-start.27
  453.2 11.1 collective-permute-start.12
  511.7 10.1 collective-permute-start.23
  532.6 9.4 collective-permute-start.26
  534.3 12.4 collective-permute-start.27
  643.2 11.2 collective-permute-start.12
  645.1 9.2 collective-permute-start.13
  701.7 10.1 collective-permute-start.23
  722.6 9.4 collective-permute-start.26
  724.2 12.4 collective-permute-start.27
  833.1 11.2 collective-permute-start.12
  835.0 9.2 collective-permute-start.13
  891.6 10.1 collective-permute-start.23
  912.5 9.4 collective-permute-start.26
  914.2 12.4 collective-permute-start.27
  1023.1 11.1 collective-permute-start.12
  1081.6 10.1 collective-permute-start.23
  1102.5 9.4 collective-permute-start.26
  1104.2 12.4 collective-permute-start.27
  1213.1 11.2 collective-permute-start.12
  1215.0 9.2 collective-permute-start.13
  1271.6 10.1 collective-permute-start.23
  1292.5 9.4 collective-permute-start.26
  1294.1 12.4 collective-permute-start.27
  1403.0 11.2 collective-permute-start.12
  1461.5 10.1 collective-permute-start.23
  1482.4 9.4 collective-permute-start.26
  1484.1 12.4 collective-permute-start.27
  1593.0 11.1 collective-permute-start.12
  1651.5 10.1 collective-permute-start.23
  1672.4 9.4 collective-permute-start.26
  1674.1 12.4 collective-permute-start.27
  1783.0 11.2 collective-permute-start.12
  1784.9 9.2 collective-permute-start.13
  1841.4 10.1 collective-permute-start.23
  1862.4 9.4 collective-permute-start.26
  1864.0 12.4 collective-permute-start.27
  1972.9 11.2 collective-permute-start.12
  2031.4 10.1 collective-permute-start.23
  2052.3 9.4 collective-permute-start.26
  2054.0 12.4 collective-permute-start.27
  (337 other events, 2889.5 us)
where the time goes:
time: 2110 us; the launch traced here: 2100 us
  starting transfers between devices  946 us (45%)
  waiting for transfers between devices  936 us (44%)
  other arithmetic  107 us (5%)
  local copies, waits for them, and re-layouts  57.7 us (3%)
  matrix products  41.6 us (2%)
    ppermute x176, waiting for transfers between devices, extended(): lax.ppermute(lax.slice_in_dim(block, block.shape[dim] - width, None, axis...  596 us
    ppermute x176, starting transfers between devices, extended(): lax.ppermute(lax.slice_in_dim(block, block.shape[dim] - width, None, axis...  572 us
    ppermute x176, starting transfers between devices, extended(): lax.ppermute(lax.slice_in_dim(block, 0, width, axis=dim), axis, backward)  353 us
    ppermute x176, waiting for transfers between devices, extended(): lax.ppermute(lax.slice_in_dim(block, 0, width, axis=dim), axis, backward)  291 us
    ppermute x11, waiting for transfers between devices, shifted(): return lax.ppermute(array, axis, pairs)  49.2 us
  transfers between devices with their start and end apart: 363, of which 264 were waited for; matrix products, arithmetic and copies ran while one was open for 5% of the time, Pallas kernels for 0%

commit v1 on v0

v1 whole, which is shorter than its diff:
```python
import jax
import jax.numpy as jnp
from jax import lax
from jax.experimental import pallas as pl
from jax.experimental.pallas import tpu as pltpu
from jax.sharding import PartitionSpec as P

AXES = ("sec", "gx", "gy")
ROWS = 160
BLK = 20
TOP = 8
DEPTHS = 4
NV = 64


def flat(x, y, zh, zl, core):
    return ((zl * 2 + core) * 8 + x * 2 + zh) * 4 + y


def half_x(half, xq):
    return xq if half == 0 else 3 - xq


def groups_of_half():
    return [
        [
            flat(half_x(half, xq), y, zh, zl, core)
            for xq in range(2)
            for zh in range(2)
            for zl in range(2)
            for y in range(4)
        ]
        for half in range(2)
        for core in range(2)
    ]


def all_devices():
    for x in range(4):
        for y in range(4):
            for zh in range(2):
                for zl in range(2):
                    for core in range(2):
                        yield x, y, zh, zl, core


def core_pairs():
    return [(flat(*d), flat(*d[:4], 1 - d[4])) for d in all_devices()]


def half_pairs():
    return [(flat(*d), flat(3 - d[0], *d[1:])) for d in all_devices()]


def kernel(place, recv, halo, vel_other, halo_vel_other, table, out, nat, natv, term, img):
    half = place[0]
    core = place[1]
    lane = lax.broadcasted_iota(jnp.int32, (8, 128), 1)
    sub = lax.broadcasted_iota(jnp.int32, (8, 128), 0)
    quarter = lane // 32
    first = lane == 0
    last = lane == 127

    def interleave(chunks):
        res = []
        for v in range(4):
            idx = (lane % 32) * 4 + v
            got = [jnp.take_along_axis(c, idx, axis=1, mode="promise_in_bounds") for c in chunks]
            res.append(
                jnp.where(
                    quarter < 2,
                    jnp.where(quarter == 0, got[0], got[1]),
                    jnp.where(quarter == 2, got[2], got[3]),
                )
            )
        return res

    def place_rows(load, dst, lead, row0, convert):
        for rg in range(4):
            vs = interleave([load(y, rg) for y in range(4)])
            for v in range(4):
                val = vs[v].astype(jnp.int32) if convert else vs[v]
                dst[lead, v, pl.ds(pl.multiple_of(row0 + rg * 8, 8), 8), :] = val

    def tile_row(xq, zh):
        return jnp.where(half == 0, 2 * xq + zh, 3 - 2 * xq + zh) * 32

    @pl.loop(0, 8)
    def _(n):
        xq, zh, zl = n // 4, (n // 2) % 2, n % 2
        row0 = tile_row(xq, zh)
        place_rows(lambda y, rg: recv[n * 4 + y, 0, pl.ds(rg * 8, 8), :], nat, zl, row0, False)
        place_rows(
            lambda y, rg: recv[n * 4 + y, 1, pl.ds(rg * 8, 8), :], natv, zl * 2 + core, row0, True
        )
        place_rows(
            lambda y, rg: vel_other[n * 4 + y, pl.ds(rg * 8, 8), :],
            natv,
            zl * 2 + 1 - core,
            row0,
            True,
        )

    @pl.loop(0, 2)
    def _(zl):
        row0 = jnp.where(half == 0, 128, 0)
        place_rows(lambda y, rg: halo[zl * 4 + y, 0, pl.ds(rg * 8, 8), :], nat, zl, row0, False)
        place_rows(
            lambda y, rg: halo[zl * 4 + y, 1, pl.ds(rg * 8, 8), :], natv, zl * 2 + core, row0, True
        )
        place_rows(
            lambda y, rg: halo_vel_other[zl * 4 + y, pl.ds(rg * 8, 8), :],
            natv,
            zl * 2 + 1 - core,
            row0,
            True,
        )

    for part in range(2):
        for i in range(BLK):
            for v in range(4):
                term[0, part, i, v] = nat[part, v, pl.ds(i, 8, stride=BLK), :]

    def across(x):
        right = jnp.where(last, 0.0, pltpu.roll(x[0], 127, 1))
        left = jnp.where(first, 0.0, pltpu.roll(x[3], 1, 1))
        q = [x[0] + x[1], x[1] + x[2], x[2] + x[3]]
        return [(left + x[0]) + q[0], q[0] + q[1], q[1] + q[2], q[2] + (x[3] + right)]

    def apply(part, source, finish):
        def row(i):
            return [term[source, part, i, v] for v in range(4)]

        h_low = [jnp.where(sub == 0, 0.0, pltpu.roll(h, 1, 0)) for h in across(row(BLK - 1))]
        h_cur = across(row(0))
        h_high = [jnp.where(sub == 7, 0.0, pltpu.roll(h, 7, 0)) for h in h_cur]
        pair = [a + b for a, b in zip(h_low, h_cur)]
        for i in range(BLK):
            h_next = across(row(i + 1)) if i < BLK - 1 else h_high
            pair_next = [a + b for a, b in zip(h_cur, h_next)]
            for v in range(4):
                finish(i, v, pair[v] + pair_next[v])
            pair, h_cur = pair_next, h_next

    @pl.loop(0, DEPTHS)
    def _(depth):
        for part in range(2):

            def first_term(i, v, s):
                term[1, part, i, v] = 0.125 * s - term[0, part, i, v]

            apply(part, 0, first_term)

        @pl.loop(1, TOP)
        def _(k):
            for part in range(2):

                def next_term(i, v, s):
                    cur = term[k, part, i, v]
                    term[k + 1, part, i, v] = (0.25 * s - cur) - (cur + term[k - 1, part, i, v])

                apply(part, k, next_term)

        @pl.loop(0, BLK)
        def _(i):
            for v in range(4):
                idx = natv[depth, v, pl.ds(i, 8, stride=BLK), :]
                real = imag = None
                for k in range(TOP + 1):
                    c_re = jnp.take_along_axis(table[2 * k], idx, axis=1, mode="promise_in_bounds")
                    c_im = jnp.take_along_axis(
                        table[2 * k + 1], idx, axis=1, mode="promise_in_bounds"
                    )
                    t_re = term[k, 0, i, v]
                    t_im = term[k, 1, i, v]
                    re = c_re * t_re - c_im * t_im
                    im = c_re * t_im + c_im * t_re
                    real = re if real is None else real + re
                    imag = im if imag is None else imag + im
                term[0, 0, i, v] = real
                term[0, 1, i, v] = imag
                img[v, pl.ds(i, 8, stride=BLK), :] = real

        slot = jnp.where(depth % 2 == core, 0, 1)
        zl = depth // 2

        @pl.loop(0, 4)
        def _(n):
            xq, zh = n // 2, n % 2
            row0 = tile_row(xq, zh)
            for rg in range(4):
                vals = [
                    img[v, pl.ds(pl.multiple_of(row0 + rg * 8, 8), 8), :] for v in range(4)
                ]
                for y in range(4):
                    idx = 32 * y + lane // 4
                    got = [
                        jnp.take_along_axis(c, idx, axis=1, mode="promise_in_bounds") for c in vals
                    ]
                    rem = lane % 4
                    res = jnp.where(
                        rem < 2,
                        jnp.where(rem == 0, got[0], got[1]),
                        jnp.where(rem == 2, got[2], got[3]),
                    )
                    out[slot, (n * 2 + zl) * 4 + y, pl.ds(rg * 8, 8), :] = res


def extrapolate(place, recv, halo, vel_other, halo_vel_other, table):
    vmem = pl.BlockSpec(memory_space=pltpu.VMEM)
    return pl.pallas_call(
        kernel,
        out_shape=jax.ShapeDtypeStruct((2, 32, 32, 128), jnp.float32),
        in_specs=[pl.BlockSpec(memory_space=pltpu.SMEM)] + [vmem] * 5,
        out_specs=vmem,
        scratch_shapes=[
            pltpu.VMEM((2, 4, ROWS, 128), jnp.float32),
            pltpu.VMEM((DEPTHS, 4, ROWS, 128), jnp.int32),
            pltpu.VMEM((TOP + 1, 2, BLK, 4, 8, 128), jnp.float32),
            pltpu.VMEM((4, ROWS, 128), jnp.float32),
        ],
        compiler_params=pltpu.CompilerParams(vmem_limit_bytes=40 * 1024 * 1024),
        cost_estimate=pl.CostEstimate(flops=70_000_000, bytes_accessed=4_000_000, transcendentals=0),
    )(place, recv, halo, vel_other, halo_vel_other, table)


def per_device(surface, coef_table, vel_index):
    sec = lax.axis_index("sec")
    gx = lax.axis_index("gx")
    gy = lax.axis_index("gy")
    zl, core = sec // 2, sec % 2
    x, zh = gx // 2, gx % 2
    half = x // 2
    xq = jnp.where(half == 0, x, 3 - x)
    freq = core * 32 + ((xq * 2 + zh) * 2 + zl) * 4 + gy
    place = jnp.stack([half, core]).astype(jnp.int32)

    with jax.named_scope("pack"):
        mine = lax.dynamic_slice(surface, (core * 32, zl, 0, 0), (32, 1, 32, 128))
        vel = jnp.broadcast_to(vel_index.astype(jnp.float32)[None], (32, 1, 32, 128))
        send = jnp.concatenate([mine, vel], axis=1)
        table = lax.dynamic_slice(coef_table, (freq, 0, 0, 0), (1, TOP + 1, 2, NV))
        table = jnp.pad(table.reshape(2 * (TOP + 1), 1, NV), ((0, 0), (0, 0), (0, 128 - NV)))
        table = jnp.broadcast_to(table, (2 * (TOP + 1), 8, 128))
    with jax.named_scope("spread"):
        recv = lax.all_to_all(send, AXES, 0, 0, axis_index_groups=groups_of_half())
    with jax.named_scope("halo"):
        edge = lax.dynamic_slice(
            recv.reshape(2, 2, 8, 2, 32, 128), (1, 1 - half, 0, 0, 0, 0), (1, 1, 8, 2, 32, 128)
        ).reshape(8, 2, 32, 128)
        halo = lax.ppermute(edge, AXES, half_pairs())
    with jax.named_scope("velocity"):
        vel_other = lax.ppermute(recv[:, 1], AXES, core_pairs())
        halo_vel_other = lax.ppermute(halo[:, 1], AXES, core_pairs())
    with jax.named_scope("extrapolate"):
        out = extrapolate(place, recv, halo, vel_other, halo_vel_other, table)
    with jax.named_scope("image"):
        total = out[0] + lax.ppermute(out[1], AXES, core_pairs())
        parts = lax.all_to_all(total, AXES, 0, 0, axis_index_groups=groups_of_half())
        return jnp.sum(parts, axis=0, keepdims=True)


def solution(mesh):
    in_specs = (P(None, None, "gx", "gy"), P(), P("sec", "gx", "gy"))
    out_specs = P("sec", "gx", "gy")
    return jax.shard_map(
        per_device, mesh=mesh, in_specs=in_specs, out_specs=out_specs, check_vma=False
    )
```

time: 2110 us -> 85.5 us (0.04)
  the two profiles are of different devices: /device:TPU:62 before, /device:TPU:0 now
where the time goes in v1:
time: 85.5 us; the launch traced here: 85.2 us
  Pallas kernels  27.5 us (32%)
  waiting for transfers between devices  24.1 us (28%)
  blocking collectives  17.1 us (20%)
  starting transfers between devices  11.9 us (14%)
  other arithmetic  2.74 us (3%)
  local copies, waits for them, and re-layouts  1.67 us (2%)
    pallas_call x1, Pallas kernels, extrapolate(): pl.pallas_call(kernel, out_shape=jax.ShapeDtypeStruct((2, 32, 32, 128), j...  27.5 us
    all_to_all x1, blocking collectives, per_device(): lax.all_to_all(total, AXES, 0, 0, axis_index_groups=groups_of_half())  17.1 us
    all_to_all x1, waiting for transfers between devices, per_device(): recv = lax.all_to_all(send, AXES, 0, 0, axis_index_groups=groups_of_half())  16.5 us
    all_to_all x1, starting transfers between devices, per_device(): recv = lax.all_to_all(send, AXES, 0, 0, axis_index_groups=groups_of_half())  9.34 us
    ppermute x1, waiting for transfers between devices, per_device(): halo = lax.ppermute(edge, AXES, half_pairs())  4.64 us
    ppermute x1, starting transfers between devices, per_device(): halo = lax.ppermute(edge, AXES, half_pairs())  2.18 us
    ppermute x1, waiting for transfers between devices, per_device(): total = out[0] + lax.ppermute(out[1], AXES, core_pairs())  1.76 us
  transfers between devices with their start and end apart: 5, of which 4 were waited for; matrix products, arithmetic and copies ran while one was open for 1% of the time, Pallas kernels for 0%

profile of v1, /device:TPU:0, one launch (start us, length us, event | category | flops | bytes accessed | tf_op | source)
XLA Modules:
  0.0 85.2 jit_solution(593501603661143268)
XLA Ops:
  0.0 0.0 copy-start
  0.0 0.9 %convert_bitcast_fusion = f32[32,128]{1,0:T(8,128)S(1)} fusion(s32[1,32,128]{2,1,0:T(8,128)} %param.5), kind=kLoop, calls=%fused_computation.7 | loop fusion | flops 4096 | bytes 32768 | tf_op jit(solution)/shard_map/pack/broadcast_in_dim | solution.py:240
  0.9 0.7 copy-done
  1.7 0.1 broadcast_in_dim.19
  1.7 1.1 %pad_maximum_fusion = f32[32,2,32,128]{3,2,1,0:T(8,128)} fusion(f32[32,1,32,128]{3,2,1,0:T(8,128)S(1)} %broadcast_in_dim.19, f32[32,1,32,128]{3,2,1,0:T(8,128)S(1)} %constant_dynamic-slice_fusion.2), kind=kLoop, calls=%fused_computation | loop fusion | flops 262144 | bytes 2097152 | tf_op jit(solution)/shard_map/pack/concatenate | solution.py:241
  2.8 9.3 %all-to-all-start = ((f32[32,2,32,128]{3,2,1,0:T(8,128)}), f32[32,2,32,128]{3,2,1,0:T(8,128)S(1)}, u32[]{:S(2)}, u32[]{:S(2)}) async-start(f32[32,2,32,128]{3,2,1,0:T(8,128)} %pad_maximum_fusion), calls=%async_computation | async-start | bytes 2097152 | tf_op jit(solution)/shard_map/spread/all_to_all | solution.py:246
  12.2 16.5 %all-to-all-done.recv = f32[32,2,32,128]{3,2,1,0:T(8,128)S(1)} async-done(((f32[32,2,32,128]{3,2,1,0:T(8,128)}), f32[32,2,32,128]{3,2,1,0:T(8,128)S(1)}, u32[]{:S(2)}, u32[]{:S(2)}) %all-to-all-start) | async-done | bytes 1048608 | tf_op jit(solution)/shard_map/spread/all_to_all | solution.py:246
  28.7 2.2 %collective-permute-start = (f32[8,2,32,128]{3,2,0,1:T(8,128)S(1)}, f32[8,2,32,128]{3,2,0,1:T(8,128)S(1)}, u32[]{:S(2)}, u32[]{:S(2)}) collective-permute-start(f32[8,2,32,128]{3,2,0,1:T(8,128)S(1)} %copy_bitcast_fusion), channel_id=1, source_target_pairs={{0,24},{32,56},{64,88},{96,120},{4,28},{36,60},{68,92},{100,124},{... | collective-permute-start | bytes 786440 | tf_op jit(solution)/shard_map/halo/ppermute | solution.py:251
  30.9 0.1 collective-permute-start.1
  31.0 0.7 constant_dynamic-slice_fusion
  31.7 4.6 %collective-permute-done = f32[8,2,32,128]{3,2,0,1:T(8,128)S(1)} collective-permute-done((f32[8,2,32,128]{3,2,0,1:T(8,128)S(1)}, f32[8,2,32,128]{3,2,0,1:T(8,128)S(1)}, u32[]{:S(2)}, u32[]{:S(2)}) %collective-permute-start) | collective-permute-done | bytes 262176 | tf_op jit(solution)/shard_map/halo/ppermute | solution.py:251
  36.3 0.1 collective-permute-start.2
  36.4 0.1 pad_add_fusion.place
  36.6 1.2 %collective-permute-done.2.halo_vel_other = f32[8,32,128]{2,1,0:T(8,128)S(1)} collective-permute-done((f32[8,32,128]{2,1,0:T(8,128)S(1)}, f32[8,32,128]{2,1,0:T(8,128)S(1)}, u32[]{:S(2)}, u32[]{:S(2)}) %collective-permute-start.2) | collective-permute-done | bytes 131104 | tf_op jit(solution)/shard_map/velocity/ppermute | solution.py:254
  37.8 0.0 collective-permute-done.1.vel_other
  37.8 27.5 %extrapolate.1 = f32[2,32,32,128]{3,2,1,0:T(8,128)S(1)} custom-call(s32[2]{0:T(128)S(1)} %pad_add_fusion.place, f32[32,2,32,128]{3,2,1,0:T(8,128)S(1)} %all-to-all-done.recv, f32[8,2,32,128]{3,2,1,0:T(8,128)S(1)} %copy.14.halo, f32[32,32,128]{2,1,0:T(8,128)S(1)} %collective-permute-done.1.vel_other, f32[8,32,128]{2,1,0:T(8,128)S(1)} %collective-permute-done.2.halo_vel_other, ...), custom_call_target="tpu_custom_call" | custom-call | flops 70000000 | bytes 4000000 | tf_op jit(solution)/shard_map/extrapolate/pallas_call | solution.py:211
  65.4 0.2 collective-permute-start.3
  65.6 1.8 %collective-permute-done.3 = f32[32,32,128]{2,1,0:T(8,128)S(1)} collective-permute-done((f32[32,32,128]{2,1,0:T(8,128)S(1)}, f32[32,32,128]{2,1,0:T(8,128)S(1)}, u32[]{:S(2)}, u32[]{:S(2)}) %collective-permute-start.3) | collective-permute-done | bytes 524320 | tf_op jit(solution)/shard_map/image/ppermute | solution.py:258
  67.3 0.1 fusion
  67.4 17.1 %all_to_all.10 = f32[32,32,128]{2,1,0:T(8,128)S(1)} all-to-all(f32[32,32,128]{2,1,0:T(8,128)S(1)} %fusion), channel_id=1, replica_groups={{0,1,2,3,64,65,66,67,4,5,6,7,68,69,70,71,8,9,10,11,72,73,74,75,12,13,14..., dimensions={0} | all-to-all | bytes 1048576 | tf_op jit(solution)/shard_map/image/all_to_all | solution.py:259
  84.5 0.6 reduce_sum.9
  (9 shorter events, 0.2 us)
Async XLA Ops:
  0.0 1.6 %copy-start = (f32[64,2,32,128]{3,2,1,0:T(8,128)S(1)}, f32[64,2,32,128]{3,2,1,0:T(8,128)}, u32[]{:S(2)}) copy-start(f32[64,2,32,128]{3,2,1,0:T(8,128)} %param.3) | copy-start | bytes 6291460
  2.8 25.9 %all-to-all-start = ((f32[32,2,32,128]{3,2,1,0:T(8,128)}), f32[32,2,32,128]{3,2,1,0:T(8,128)S(1)}, u32[]{:S(2)}, u32[]{:S(2)}) async-start(f32[32,2,32,128]{3,2,1,0:T(8,128)} %pad_maximum_fusion), calls=%async_computation | async-start | bytes 2097152 | tf_op jit(solution)/shard_map/spread/all_to_all | solution.py:246
  28.7 7.7 %collective-permute-start = (f32[8,2,32,128]{3,2,0,1:T(8,128)S(1)}, f32[8,2,32,128]{3,2,0,1:T(8,128)S(1)}, u32[]{:S(2)}, u32[]{:S(2)}) collective-permute-start(f32[8,2,32,128]{3,2,0,1:T(8,128)S(1)} %copy_bitcast_fusion), channel_id=1, source_target_pairs={{0,24},{32,56},{64,88},{96,120},{4,28},{36,60},{68,92},{100,124},{... | collective-permute-start | bytes 786440 | tf_op jit(solution)/shard_map/halo/ppermute | solution.py:251
  30.9 6.9 %collective-permute-start.1 = (f32[32,32,128]{2,1,0:T(8,128)S(1)}, f32[32,32,128]{2,1,0:T(8,128)S(1)}, u32[]{:S(2)}, u32[]{:S(2)}) collective-permute-start(f32[32,32,128]{2,1,0:T(8,128)S(1)} %slice_bitcast_fusion.2), channel_id=1, source_target_pairs={{0,32},{32,0},{64,96},{96,64},{4,36},{36,4},{68,100},{100,68},{1,3... | collective-permute-start | bytes 1572872 | tf_op jit(solution)/shard_map/velocity/ppermute | solution.py:253
  36.3 1.4 %collective-permute-start.2 = (f32[8,32,128]{2,1,0:T(8,128)S(1)}, f32[8,32,128]{2,1,0:T(8,128)S(1)}, u32[]{:S(2)}, u32[]{:S(2)}) collective-permute-start(f32[8,32,128]{2,1,0:T(8,128)S(1)} %slice_bitcast_fusion.3), channel_id=1, source_target_pairs={{0,32},{32,0},{64,96},{96,64},{4,36},{36,4},{68,100},{100,68},{1,3... | collective-permute-start | bytes 393224 | tf_op jit(solution)/shard_map/velocity/ppermute | solution.py:254
  65.4 2.0 %collective-permute-start.3 = (f32[32,32,128]{2,1,0:T(8,128)S(1)}, f32[32,32,128]{2,1,0:T(8,128)S(1)}, u32[]{:S(2)}, u32[]{:S(2)}) collective-permute-start(f32[32,32,128]{2,1,0:T(8,128)S(1)} %slice_bitcast_fusion), channel_id=1, source_target_pairs={{0,32},{32,0},{64,96},{96,64},{4,36},{36,4},{68,100},{100,68},{1,3... | collective-permute-start | bytes 1572872 | tf_op jit(solution)/shard_map/image/ppermute | solution.py:258

commit v2 on v1

--- a/solution.py
+++ b/solution.py
@@ -11,6 +11,7 @@
 TOP = 8
 DEPTHS = 4
 NV = 64
+COEFS = 2 * (TOP + 1)
 
 
 def flat(x, y, zh, zl, core):
@@ -52,32 +53,120 @@
     return [(flat(*d), flat(3 - d[0], *d[1:])) for d in all_devices()]
 
 
-def kernel(place, recv, halo, vel_other, halo_vel_other, table, out, nat, natv, term, img):
-    half = place[0]
-    core = place[1]
-    lane = lax.broadcasted_iota(jnp.int32, (8, 128), 1)
+def gather_lanes(x, idx):
+    return jnp.take_along_axis(x, idx, axis=1, mode="promise_in_bounds")
+
+
+def lanes():
+    return lax.broadcasted_iota(jnp.int32, (8, 128), 1)
+
+
+def swap_blocks(x):
+    lane = lanes()
+    low = lane < 64
+    even = (lane // 32) % 2 == 0
+    near = [jnp.where(low, x[i], pltpu.roll(x[i + 2], 64, 1)) for i in range(2)]
+    far = [jnp.where(low, pltpu.roll(x[i], 64, 1), x[i + 2]) for i in range(2)]
+    res = []
+    for a, b in (near, far):
+        res.append(jnp.where(even, a, pltpu.roll(b, 32, 1)))
+        res.append(jnp.where(even, pltpu.roll(a, 96, 1), b))
+    return res
+
+
+def coordinates():
+    sec, gx = lax.axis_index("sec"), lax.axis_index("gx")
+    x, zh = gx // 2, gx % 2
+    return x, zh, sec // 2, sec % 2
+
+
+def pack_kernel(surface, vel, send, buf, vel_buf, sems):
+    _, _, zl, core = coordinates()
+    lane = lanes()
+    idx = 4 * (lane % 32) + lane // 32
+    vel_copy = pltpu.make_async_copy(vel, vel_buf, sems.at[4])
+    vel_copy.start()
+    copies = [
+        pltpu.make_async_copy(
+            surface.at[pl.ds(core * 32 + j * 8, 8), zl], buf.at[pl.ds(j * 8, 8)], sems.at[j]
+        )
+        for j in range(4)
+    ]
+    for copy in copies:
+        copy.start()
+    vel_copy.wait()
+    rows = [
+        gather_lanes(vel_buf[0, pl.ds(rg * 8, 8), :].astype(jnp.float32), idx) for rg in range(4)
+    ]
+
+    @pl.loop(0, 32)
+    def _(n):
+        for rg in range(4):
+            send[n, 1, pl.ds(rg * 8, 8), :] = rows[rg]
+
+    for j, copy in enumerate(copies):
+        copy.wait()
+
+        @pl.loop(0, 2)
+        def _(m):
+            for u in range(4):
+                n = j * 8 + m * 4 + u
+                for rg in range(4):
+                    send[n, 0, pl.ds(rg * 8, 8), :] = gather_lanes(
+                        buf[n, pl.ds(rg * 8, 8), :], idx
+                    )
+
+
+def pack(surface, vel):
+    vmem = pl.BlockSpec(memory_space=pltpu.VMEM)
+    return pl.pallas_call(
+        pack_kernel,
+        out_shape=jax.ShapeDtypeStruct((32, 2, 32, 128), jnp.float32),
+        in_specs=[pl.BlockSpec(memory_space=pl.ANY)] * 2,
+        out_specs=vmem,
+        scratch_shapes=[
+            pltpu.VMEM((32, 32, 128), jnp.float32),
+            pltpu.VMEM((1, 32, 128), jnp.int32),
+            pltpu.SemaphoreType.DMA((5,)),
+        ],
+        compiler_params=pltpu.CompilerParams(vmem_limit_bytes=60 * 1024 * 1024),
+    )(surface, vel)
+
+
+def sum_kernel(parts, image):
+    lane = lanes()
+    idx = 32 * (lane % 4) + lane // 4
+    for rg in range(4):
+        terms = [parts[n, pl.ds(rg * 8, 8), :] for n in range(32)]
+        while len(terms) > 1:
+            terms = [a + b for a, b in zip(terms[::2], terms[1::2])]
+        image[0, pl.ds(rg * 8, 8), :] = gather_lanes(terms[0], idx)
+
+
+def add_up(parts):
+    vmem = pl.BlockSpec(memory_space=pltpu.VMEM)
+    return pl.pallas_call(
+        sum_kernel,
+        out_shape=jax.ShapeDtypeStruct((1, 32, 128), jnp.float32),
+        in_specs=[vmem],
+        out_specs=vmem,
+        compiler_params=pltpu.CompilerParams(vmem_limit_bytes=16 * 1024 * 1024),
+    )(parts)
+
+
+def kernel(
+    recv, halo, halo_vel, vel_other, halo_vel_other, table, out, nat, natv, term, img
+):
+    x, _, _, core = coordinates()
+    half = x // 2
+    lane = lanes()
     sub = lax.broadcasted_iota(jnp.int32, (8, 128), 0)
-    quarter = lane // 32
     first = lane == 0
     last = lane == 127
 
-    def interleave(chunks):
-        res = []
-        for v in range(4):
-            idx = (lane % 32) * 4 + v
-            got = [jnp.take_along_axis(c, idx, axis=1, mode="promise_in_bounds") for c in chunks]
-            res.append(
-                jnp.where(
-                    quarter < 2,
-                    jnp.where(quarter == 0, got[0], got[1]),
-                    jnp.where(quarter == 2, got[2], got[3]),
-                )
-            )
-        return res
-
     def place_rows(load, dst, lead, row0, convert):
         for rg in range(4):
-            vs = interleave([load(y, rg) for y in range(4)])
+            vs = swap_blocks([load(y, rg) for y in range(4)])
             for v in range(4):
                 val = vs[v].astype(jnp.int32) if convert else vs[v]
                 dst[lead, v, pl.ds(pl.multiple_of(row0 + rg * 8, 8), 8), :] = val
@@ -101,20 +190,19 @@
             True,
         )
 
-    @pl.loop(0, 2)
-    def _(zl):
-        row0 = jnp.where(half == 0, 128, 0)
-        place_rows(lambda y, rg: halo[zl * 4 + y, 0, pl.ds(rg * 8, 8), :], nat, zl, row0, False)
-        place_rows(
-            lambda y, rg: halo[zl * 4 + y, 1, pl.ds(rg * 8, 8), :], natv, zl * 2 + core, row0, True
-        )
-        place_rows(
-            lambda y, rg: halo_vel_other[zl * 4 + y, pl.ds(rg * 8, 8), :],
-            natv,
-            zl * 2 + 1 - core,
-            row0,
-            True,
-        )
+    edge = jnp.where(half == 0, 128, 0)
+    natv[:, :, pl.ds(pl.multiple_of(edge, 8), 32), :] = jnp.zeros((DEPTHS, 4, 32, 128), jnp.int32)
+    for part in range(2):
+        place_rows(lambda y, rg: halo[part * 4 + y, pl.ds(rg * 8, 8), :], nat, part, edge, False)
+
+    for ref, parity in ((halo_vel, core), (halo_vel_other, 1 - core)):
+        for rg in range(4):
+            vs = swap_blocks([ref[y, pl.ds(rg * 8, 8), :] for y in range(4)])
+            first_row = jnp.where(half == 0, 128, 8) + rg * 8
+            row0 = first_row if rg < 3 else jnp.where(half == 0, 128, 24)
+            depth = parity if rg < 3 else 2 + parity
+            for v in range(4):
+                natv[depth, v, pl.ds(pl.multiple_of(row0, 8), 8), :] = vs[v].astype(jnp.int32)
 
     for part in range(2):
         for i in range(BLK):
@@ -161,16 +249,14 @@
 
                 apply(part, k, next_term)
 
-        @pl.loop(0, BLK)
+        @pl.loop(0, BLK, unroll=10)
         def _(i):
             for v in range(4):
                 idx = natv[depth, v, pl.ds(i, 8, stride=BLK), :]
                 real = imag = None
                 for k in range(TOP + 1):
-                    c_re = jnp.take_along_axis(table[2 * k], idx, axis=1, mode="promise_in_bounds")
-                    c_im = jnp.take_along_axis(
-                        table[2 * k + 1], idx, axis=1, mode="promise_in_bounds"
-                    )
+                    c_re = gather_lanes(table[2 * k], idx)
+                    c_im = gather_lanes(table[2 * k + 1], idx)
                     t_re = term[k, 0, i, v]
                     t_im = term[k, 1, i, v]
                     re = c_re * t_re - c_im * t_im
@@ -184,34 +270,24 @@
         slot = jnp.where(depth % 2 == core, 0, 1)
         zl = depth // 2
 
-        @pl.loop(0, 4)
+        @pl.loop(0, 4, unroll=4)
         def _(n):
             xq, zh = n // 2, n % 2
             row0 = tile_row(xq, zh)
             for rg in range(4):
-                vals = [
-                    img[v, pl.ds(pl.multiple_of(row0 + rg * 8, 8), 8), :] for v in range(4)
-                ]
+                vals = swap_blocks(
+                    [img[v, pl.ds(pl.multiple_of(row0 + rg * 8, 8), 8), :] for v in range(4)]
+                )
                 for y in range(4):
-                    idx = 32 * y + lane // 4
-                    got = [
-                        jnp.take_along_axis(c, idx, axis=1, mode="promise_in_bounds") for c in vals
-                    ]
-                    rem = lane % 4
-                    res = jnp.where(
-                        rem < 2,
-                        jnp.where(rem == 0, got[0], got[1]),
-                        jnp.where(rem == 2, got[2], got[3]),
-                    )
-                    out[slot, (n * 2 + zl) * 4 + y, pl.ds(rg * 8, 8), :] = res
-
-
-def extrapolate(place, recv, halo, vel_other, halo_vel_other, table):
+                    out[slot, (n * 2 + zl) * 4 + y, pl.ds(rg * 8, 8), :] = vals[y]
+
+
+def extrapolate(*operands):
     vmem = pl.BlockSpec(memory_space=pltpu.VMEM)
     return pl.pallas_call(
         kernel,
         out_shape=jax.ShapeDtypeStruct((2, 32, 32, 128), jnp.float32),
-        in_specs=[pl.BlockSpec(memory_space=pltpu.SMEM)] + [vmem] * 5,
+        in_specs=[vmem] * 6,
         out_specs=vmem,
         scratch_shapes=[
             pltpu.VMEM((2, 4, ROWS, 128), jnp.float32),
@@ -221,7 +297,7 @@
         ],
         compiler_params=pltpu.CompilerParams(vmem_limit_bytes=40 * 1024 * 1024),
         cost_estimate=pl.CostEstimate(flops=70_000_000, bytes_accessed=4_000_000, transcendentals=0),
-    )(place, recv, halo, vel_other, halo_vel_other, table)
+    )(*operands)
 
 
 def per_device(surface, coef_table, vel_index):
@@ -233,31 +309,38 @@
     half = x // 2
     xq = jnp.where(half == 0, x, 3 - x)
     freq = core * 32 + ((xq * 2 + zh) * 2 + zl) * 4 + gy
-    place = jnp.stack([half, core]).astype(jnp.int32)
 
     with jax.named_scope("pack"):
-        mine = lax.dynamic_slice(surface, (core * 32, zl, 0, 0), (32, 1, 32, 128))
-        vel = jnp.broadcast_to(vel_index.astype(jnp.float32)[None], (32, 1, 32, 128))
-        send = jnp.concatenate([mine, vel], axis=1)
-        table = lax.dynamic_slice(coef_table, (freq, 0, 0, 0), (1, TOP + 1, 2, NV))
-        table = jnp.pad(table.reshape(2 * (TOP + 1), 1, NV), ((0, 0), (0, 0), (0, 128 - NV)))
-        table = jnp.broadcast_to(table, (2 * (TOP + 1), 8, 128))
+        send = pack(surface, vel_index)
     with jax.named_scope("spread"):
         recv = lax.all_to_all(send, AXES, 0, 0, axis_index_groups=groups_of_half())
     with jax.named_scope("halo"):
         edge = lax.dynamic_slice(
             recv.reshape(2, 2, 8, 2, 32, 128), (1, 1 - half, 0, 0, 0, 0), (1, 1, 8, 2, 32, 128)
         ).reshape(8, 2, 32, 128)
-        halo = lax.ppermute(edge, AXES, half_pairs())
+        edge_vel = jnp.concatenate(
+            [
+                lax.dynamic_slice(edge, (0, 1, 8 * (1 - half), 0), (4, 1, 24, 128))[:, 0],
+                lax.dynamic_slice(edge, (4, 1, 24 * (1 - half), 0), (4, 1, 8, 128))[:, 0],
+            ],
+            axis=1,
+        )
+        halo_vel = lax.ppermute(edge_vel, AXES, half_pairs())
+        halo = lax.ppermute(edge[:, 0], AXES, half_pairs())
     with jax.named_scope("velocity"):
         vel_other = lax.ppermute(recv[:, 1], AXES, core_pairs())
-        halo_vel_other = lax.ppermute(halo[:, 1], AXES, core_pairs())
+        halo_vel_other = lax.ppermute(halo_vel, AXES, core_pairs())
+    with jax.named_scope("tables"):
+        own = lax.dynamic_slice(coef_table, (freq, 0, 0, 0), (1, TOP + 1, 2, NV))
+        own = own.reshape(COEFS, NV)
+        table = jnp.pad(own[:, None], ((0, 0), (0, 0), (0, 128 - NV)))
+        table = jnp.broadcast_to(table, (COEFS, 8, 128))
     with jax.named_scope("extrapolate"):
-        out = extrapolate(place, recv, halo, vel_other, halo_vel_other, table)
+        out = extrapolate(recv, halo, halo_vel, vel_other, halo_vel_other, table)
     with jax.named_scope("image"):
         total = out[0] + lax.ppermute(out[1], AXES, core_pairs())
         parts = lax.all_to_all(total, AXES, 0, 0, axis_index_groups=groups_of_half())
-        return jnp.sum(parts, axis=0, keepdims=True)
+        return add_up(parts)
 
 
 def solution(mesh):

time: 85.5 us -> 74.2 us (0.87)
  Pallas kernels: 27.5 us -> 20.4 us
  other arithmetic: 2.74 us -> 0.09 us
  local copies, waits for them, and re-layouts: 1.67 us -> 0.16 us
  blocking collectives: 17.1 us -> 16 us
  starting transfers between devices: 11.9 us -> 12.9 us
    pallas_call x1, Pallas kernels: 27.5 us -> 17 us  [extrapolate(): pl.pallas_call(kernel, out_shape=jax.ShapeDtypeStruct((2, 32, 32, 128), j...]
    pallas_call x0 -> x2, Pallas kernels: none -> 3.39 us  [the longest x1 2.67 us: pack(): pl.pallas_call(pack_kernel, out_shape=jax.ShapeDtypeStruct((32, 2, 32, 12...]
    all_to_all x1, blocking collectives: 17.1 us -> 16 us  [per_device(): lax.all_to_all(total, AXES, 0, 0, axis_index_groups=groups_of_half())]
    ppermute x2 -> x3, starting transfers between devices: 2.26 us -> 3.4 us  [the longest x1 2.18 us: per_device(): halo_vel = lax.ppermute(edge_vel, AXES, half_pairs())]
    concatenate x1, other arithmetic: 1.06 us -> 0.01 us  [per_device(): jnp.concatenate([lax.dynamic_slice(edge, (0, 1, 8 * (1 - half), 0), (4, 1...]
    broadcast_in_dim x1 -> x0, other arithmetic: 0.87 us -> none  [per_device(): jnp.broadcast_to(vel_index.astype(jnp.float32)[None], (32, 1, 32, 128))]
    ppermute x2 -> x3, waiting for transfers between devices: 5.86 us -> 5.93 us  [the longest x1 3.97 us: per_device(): halo = lax.ppermute(edge[:, 0], AXES, half_pairs())]
  transfers between devices with their start and end apart: 5 -> 6, of which waited for: 4 -> 4; matrix products, arithmetic and copies ran while one was open for 1% -> 0% of each run, Pallas kernels for 0% -> 0%
where the time goes in v2:
time: 74.2 us; the launch traced here: 74 us
  waiting for transfers between devices  24.3 us (33%)
  Pallas kernels  20.4 us (27%)
  blocking collectives  16 us (22%)
  starting transfers between devices  12.9 us (17%)
    pallas_call x1, Pallas kernels, extrapolate(): pl.pallas_call(kernel, out_shape=jax.ShapeDtypeStruct((2, 32, 32, 128), j...  17 us
    all_to_all x1, waiting for transfers between devices, per_device(): recv = lax.all_to_all(send, AXES, 0, 0, axis_index_groups=groups_of_half())  16.4 us
    all_to_all x1, blocking collectives, per_device(): lax.all_to_all(total, AXES, 0, 0, axis_index_groups=groups_of_half())  16 us
    all_to_all x1, starting transfers between devices, per_device(): recv = lax.all_to_all(send, AXES, 0, 0, axis_index_groups=groups_of_half())  9.36 us
    ppermute x1, waiting for transfers between devices, per_device(): halo = lax.ppermute(edge[:, 0], AXES, half_pairs())  3.97 us
    pallas_call x1, Pallas kernels, pack(): pl.pallas_call(pack_kernel, out_shape=jax.ShapeDtypeStruct((32, 2, 32, 12...  2.67 us
    ppermute x1, starting transfers between devices, per_device(): halo_vel = lax.ppermute(edge_vel, AXES, half_pairs())  2.18 us
    ppermute x1, waiting for transfers between devices, per_device(): halo_vel = lax.ppermute(edge_vel, AXES, half_pairs())  1.96 us
  transfers between devices with their start and end apart: 6, of which 4 were waited for; matrix products, arithmetic and copies ran while one was open for 0% of the time, Pallas kernels for 0%

profile of v2, /device:TPU:0, one launch (start us, length us, event | category | flops | bytes accessed | tf_op | source)
XLA Modules:
  0.0 74.0 jit_solution(9889897973453101796)
XLA Ops:
  0.0 0.0 copy-start
  0.0 2.7 %pack.1 = f32[32,2,32,128]{3,2,1,0:T(8,128)} custom-call(f32[64,2,32,128]{3,2,1,0:T(8,128)} %surface.1, s32[1,32,128]{2,1,0:T(8,128)} %vel.1), custom_call_target="tpu_custom_call" | custom-call | tf_op jit(solution)/shard_map/pack/pallas_call | solution.py:122
  2.7 9.4 %all-to-all-start = ((f32[32,2,32,128]{3,2,1,0:T(8,128)}), f32[32,2,32,128]{3,2,1,0:T(8,128)S(1)}, u32[]{:S(2)}, u32[]{:S(2)}) async-start(f32[32,2,32,128]{3,2,1,0:T(8,128)} %pack.1), calls=%async_computation | async-start | bytes 2097152 | tf_op jit(solution)/shard_map/spread/all_to_all | solution.py:316
  12.1 16.4 %all-to-all-done.recv = f32[32,2,32,128]{3,2,1,0:T(8,128)S(1)} async-done(((f32[32,2,32,128]{3,2,1,0:T(8,128)}), f32[32,2,32,128]{3,2,1,0:T(8,128)S(1)}, u32[]{:S(2)}, u32[]{:S(2)}) %all-to-all-start) | async-done | bytes 1048608 | tf_op jit(solution)/shard_map/spread/all_to_all | solution.py:316
  28.6 2.2 %collective-permute-start.1 = (f32[4,32,128]{2,1,0:T(8,128)S(1)}, f32[4,32,128]{2,1,0:T(8,128)S(1)}, u32[]{:S(2)}, u32[]{:S(2)}) collective-permute-start(f32[4,32,128]{2,1,0:T(8,128)S(1)} %pad_maximum_fusion), channel_id=1, source_target_pairs={{0,24},{32,56},{64,88},{96,120},{4,28},{36,60},{68,92},{100,124},{... | collective-permute-start | bytes 196616 | tf_op jit(solution)/shard_map/halo/ppermute | solution.py:328
  30.8 0.1 collective-permute-start.2
  31.0 1.2 %collective-permute-start = (f32[8,32,128]{2,1,0:T(8,128)S(1)}, f32[8,32,128]{2,1,0:T(8,128)S(1)}, u32[]{:S(2)}, u32[]{:S(2)}) collective-permute-start(f32[8,32,128]{2,1,0:T(8,128)S(1)} %slice_bitcast_fusion.3), channel_id=1, source_target_pairs={{0,24},{32,56},{64,88},{96,120},{4,28},{36,60},{68,92},{100,124},{... | collective-permute-start | bytes 393224 | tf_op jit(solution)/shard_map/halo/ppermute | solution.py:329
  32.2 0.0 copy-done
  32.2 2.0 %collective-permute-done.1.halo_vel = f32[4,32,128]{2,1,0:T(8,128)S(1)} collective-permute-done((f32[4,32,128]{2,1,0:T(8,128)S(1)}, f32[4,32,128]{2,1,0:T(8,128)S(1)}, u32[]{:S(2)}, u32[]{:S(2)}) %collective-permute-start.1) | collective-permute-done | bytes 65568 | tf_op jit(solution)/shard_map/halo/ppermute | solution.py:328
  34.2 0.0 collective-permute-start.3
  34.2 4.0 %collective-permute-done.halo = f32[8,32,128]{2,1,0:T(8,128)S(1)} collective-permute-done((f32[8,32,128]{2,1,0:T(8,128)S(1)}, f32[8,32,128]{2,1,0:T(8,128)S(1)}, u32[]{:S(2)}, u32[]{:S(2)}) %collective-permute-start) | collective-permute-done | bytes 131104 | tf_op jit(solution)/shard_map/halo/ppermute | solution.py:329
  38.2 0.0 collective-permute-done.3.halo_vel_other
  38.2 0.0 collective-permute-done.2.vel_other
  38.2 17.0 %extrapolate.1 = f32[2,32,32,128]{3,2,1,0:T(8,128)S(1)} custom-call(f32[32,2,32,128]{3,2,1,0:T(8,128)S(1)} %all-to-all-done.recv, f32[8,32,128]{2,1,0:T(8,128)S(1)} %collective-permute-done.halo, f32[4,32,128]{2,1,0:T(8,128)S(1)} %collective-permute-done.1.halo_vel, f32[32,32,128]{2,1,0:T(8,128)S(1)} %collective-permute-done.2.vel_other, ...), custom_call_target="tpu_custom_call" | custom-call | flops 70000000 | bytes 4000000 | tf_op jit(solution)/shard_map/extrapolate/pallas_call | solution.py:287
  55.2 0.1 collective-permute-start.4
  55.3 1.9 %collective-permute-done.4 = f32[32,32,128]{2,1,0:T(8,128)S(1)} collective-permute-done((f32[32,32,128]{2,1,0:T(8,128)S(1)}, f32[32,32,128]{2,1,0:T(8,128)S(1)}, u32[]{:S(2)}, u32[]{:S(2)}) %collective-permute-start.4) | collective-permute-done | bytes 524320 | tf_op jit(solution)/shard_map/image/ppermute | solution.py:341
  57.2 0.1 fusion
  57.3 16.0 %all_to_all.10.parts = f32[32,32,128]{2,1,0:T(8,128)S(1)} all-to-all(f32[32,32,128]{2,1,0:T(8,128)S(1)} %fusion), channel_id=1, replica_groups={{0,1,2,3,64,65,66,67,4,5,6,7,68,69,70,71,8,9,10,11,72,73,74,75,12,13,14..., dimensions={0} | all-to-all | bytes 1048576 | tf_op jit(solution)/shard_map/image/all_to_all | solution.py:342
  73.3 0.7 image.1
  (11 shorter events, 0.2 us)
Async XLA Ops:
  0.0 32.2 %copy-start = (f32[64,9,2,64]{3,2,1,0:T(2,128)S(1)}, f32[64,9,2,64]{3,2,1,0:T(2,128)}, u32[]{:S(2)}) copy-start(f32[64,9,2,64]{3,2,1,0:T(2,128)} %param.4) | copy-start | bytes 884740
  2.7 25.9 %all-to-all-start = ((f32[32,2,32,128]{3,2,1,0:T(8,128)}), f32[32,2,32,128]{3,2,1,0:T(8,128)S(1)}, u32[]{:S(2)}, u32[]{:S(2)}) async-start(f32[32,2,32,128]{3,2,1,0:T(8,128)} %pack.1), calls=%async_computation | async-start | bytes 2097152 | tf_op jit(solution)/shard_map/spread/all_to_all | solution.py:316
  28.6 5.6 %collective-permute-start.1 = (f32[4,32,128]{2,1,0:T(8,128)S(1)}, f32[4,32,128]{2,1,0:T(8,128)S(1)}, u32[]{:S(2)}, u32[]{:S(2)}) collective-permute-start(f32[4,32,128]{2,1,0:T(8,128)S(1)} %pad_maximum_fusion), channel_id=1, source_target_pairs={{0,24},{32,56},{64,88},{96,120},{4,28},{36,60},{68,92},{100,124},{... | collective-permute-start | bytes 196616 | tf_op jit(solution)/shard_map/halo/ppermute | solution.py:328
  30.8 7.3 %collective-permute-start.2 = (f32[32,32,128]{2,1,0:T(8,128)S(1)}, f32[32,32,128]{2,1,0:T(8,128)S(1)}, u32[]{:S(2)}, u32[]{:S(2)}) collective-permute-start(f32[32,32,128]{2,1,0:T(8,128)S(1)} %slice_bitcast_fusion.2), channel_id=1, source_target_pairs={{0,32},{32,0},{64,96},{96,64},{4,36},{36,4},{68,100},{100,68},{1,3... | collective-permute-start | bytes 1572872 | tf_op jit(solution)/shard_map/velocity/ppermute | solution.py:331
  31.0 7.2 %collective-permute-start = (f32[8,32,128]{2,1,0:T(8,128)S(1)}, f32[8,32,128]{2,1,0:T(8,128)S(1)}, u32[]{:S(2)}, u32[]{:S(2)}) collective-permute-start(f32[8,32,128]{2,1,0:T(8,128)S(1)} %slice_bitcast_fusion.3), channel_id=1, source_target_pairs={{0,24},{32,56},{64,88},{96,120},{4,28},{36,60},{68,92},{100,124},{... | collective-permute-start | bytes 393224 | tf_op jit(solution)/shard_map/halo/ppermute | solution.py:329
  34.2 4.0 %collective-permute-start.3 = (f32[4,32,128]{2,1,0:T(8,128)S(1)}, f32[4,32,128]{2,1,0:T(8,128)S(1)}, u32[]{:S(2)}, u32[]{:S(2)}) collective-permute-start(f32[4,32,128]{2,1,0:T(8,128)S(1)} %collective-permute-done.1.halo_vel), channel_id=1, source_target_pairs={{0,32},{32,0},{64,96},{96,64},{4,36},{36,4},{68,100},{100,68},{1,3... | collective-permute-start | bytes 196616 | tf_op jit(solution)/shard_map/velocity/ppermute | solution.py:332
  55.2 2.0 %collective-permute-start.4 = (f32[32,32,128]{2,1,0:T(8,128)S(1)}, f32[32,32,128]{2,1,0:T(8,128)S(1)}, u32[]{:S(2)}, u32[]{:S(2)}) collective-permute-start(f32[32,32,128]{2,1,0:T(8,128)S(1)} %slice_bitcast_fusion), channel_id=1, source_target_pairs={{0,32},{32,0},{64,96},{96,64},{4,36},{36,4},{68,100},{100,68},{1,3... | collective-permute-start | bytes 1572872 | tf_op jit(solution)/shard_map/image/ppermute | solution.py:341

commit v3 on v2

--- a/solution.py
+++ b/solution.py
@@ -6,8 +6,10 @@
 from jax.sharding import PartitionSpec as P
 
 AXES = ("sec", "gx", "gy")
-ROWS = 160
+OWN = 16
 BLK = 20
+PITCH = 24
+AHEAD = 3
 TOP = 8
 DEPTHS = 4
 NV = 64
@@ -99,22 +101,16 @@
         gather_lanes(vel_buf[0, pl.ds(rg * 8, 8), :].astype(jnp.float32), idx) for rg in range(4)
     ]
 
-    @pl.loop(0, 32)
-    def _(n):
+    for n in range(32):
         for rg in range(4):
             send[n, 1, pl.ds(rg * 8, 8), :] = rows[rg]
 
     for j, copy in enumerate(copies):
         copy.wait()
-
-        @pl.loop(0, 2)
-        def _(m):
-            for u in range(4):
-                n = j * 8 + m * 4 + u
-                for rg in range(4):
-                    send[n, 0, pl.ds(rg * 8, 8), :] = gather_lanes(
-                        buf[n, pl.ds(rg * 8, 8), :], idx
-                    )
+        for u in range(8):
+            n = j * 8 + u
+            for rg in range(4):
+                send[n, 0, pl.ds(rg * 8, 8), :] = gather_lanes(buf[n, pl.ds(rg * 8, 8), :], idx)
 
 
 def pack(surface, vel):
@@ -154,60 +150,111 @@
     )(parts)
 
 
-def kernel(
-    recv, halo, halo_vel, vel_other, halo_vel_other, table, out, nat, natv, term, img
-):
+def tile_group(t, rg):
+    return pl.ds(pl.multiple_of((2 * t + rg // 2) * PITCH + 8 * (rg % 2), 8), 8)
+
+
+def own_tile(half, n):
+    return jnp.where(half == 0, n, (n + 2) % 4)
+
+
+def prepare_kernel(recv, vel_other, table, start, index, coefs, zero, nat, natv):
+    zero[...] = jnp.zeros_like(zero)
+    x, _, _, core = coordinates()
+    half = x // 2
+
+    @pl.loop(0, 8)
+    def _(n):
+        t = own_tile(half, n // 2)
+        zl = n % 2
+        for rg in range(4):
+            dst = tile_group(t, rg)
+            for slab in range(2):
+                vs = swap_blocks([recv[n * 4 + y, slab, pl.ds(rg * 8, 8), :] for y in range(4)])
+                for v in range(4):
+                    if slab == 0:
+                        nat[zl, v, dst, :] = vs[v]
+                    else:
+                        natv[zl * 2 + core, v, dst, :] = vs[v].astype(jnp.int32)
+            vs = swap_blocks([vel_other[n * 4 + y, pl.ds(rg * 8, 8), :] for y in range(4)])
+            for v in range(4):
+                natv[zl * 2 + 1 - core, v, dst, :] = vs[v].astype(jnp.int32)
+
+    def block(i):
+        return pl.ds(i, 8, stride=PITCH)
+
+    for i in range(OWN):
+        for v in range(4):
+            for part in range(2):
+                start[part, i, v] = nat[part, v, block(i), :]
+            for depth in range(AHEAD, DEPTHS):
+                index[depth - AHEAD, i, v] = natv[depth, v, block(i), :]
+
+    @pl.loop(0, AHEAD)
+    def _(depth):
+        @pl.loop(0, OWN, unroll=8)
+        def _(i):
+            for v in range(4):
+                idx = natv[depth, v, block(i), :]
+                for n in range(COEFS):
+                    coefs[depth, i, v, n] = gather_lanes(table[n], idx)
+
+
+def prepare(recv, vel_other, table):
+    vmem = pl.BlockSpec(memory_space=pltpu.VMEM)
+    return pl.pallas_call(
+        prepare_kernel,
+        out_shape=(
+            jax.ShapeDtypeStruct((2, OWN, 4, 8, 128), jnp.float32),
+            jax.ShapeDtypeStruct((DEPTHS - AHEAD, OWN, 4, 8, 128), jnp.int32),
+            jax.ShapeDtypeStruct((AHEAD, OWN, 4, COEFS, 8, 128), jnp.float32),
+            jax.ShapeDtypeStruct((8, 128), jnp.float32),
+        ),
+        in_specs=[vmem] * 3,
+        out_specs=(vmem,) * 4,
+        scratch_shapes=[
+            pltpu.VMEM((2, 4, 8 * PITCH, 128), jnp.float32),
+            pltpu.VMEM((DEPTHS, 4, 8 * PITCH, 128), jnp.int32),
+        ],
+        compiler_params=pltpu.CompilerParams(vmem_limit_bytes=24 * 1024 * 1024),
+        cost_estimate=pl.CostEstimate(flops=20_000_000, bytes_accessed=4_000_000, transcendentals=0),
+    )(recv, vel_other, table)
+
+
+def kernel(start, index, coefs, halo, halo_vel_other, table, out, nat, natv, term, img):
     x, _, _, core = coordinates()
     half = x // 2
     lane = lanes()
     sub = lax.broadcasted_iota(jnp.int32, (8, 128), 0)
     first = lane == 0
     last = lane == 127
-
-    def place_rows(load, dst, lead, row0, convert):
+    before = jnp.where(half == 0, 0.0, 1.0)
+    after = 1.0 - before
+
+    for part in range(2):
         for rg in range(4):
-            vs = swap_blocks([load(y, rg) for y in range(4)])
-            for v in range(4):
-                val = vs[v].astype(jnp.int32) if convert else vs[v]
-                dst[lead, v, pl.ds(pl.multiple_of(row0 + rg * 8, 8), 8), :] = val
-
-    def tile_row(xq, zh):
-        return jnp.where(half == 0, 2 * xq + zh, 3 - 2 * xq + zh) * 32
-
-    @pl.loop(0, 8)
-    def _(n):
-        xq, zh, zl = n // 4, (n // 2) % 2, n % 2
-        row0 = tile_row(xq, zh)
-        place_rows(lambda y, rg: recv[n * 4 + y, 0, pl.ds(rg * 8, 8), :], nat, zl, row0, False)
-        place_rows(
-            lambda y, rg: recv[n * 4 + y, 1, pl.ds(rg * 8, 8), :], natv, zl * 2 + core, row0, True
-        )
-        place_rows(
-            lambda y, rg: vel_other[n * 4 + y, pl.ds(rg * 8, 8), :],
-            natv,
-            zl * 2 + 1 - core,
-            row0,
-            True,
-        )
-
-    edge = jnp.where(half == 0, 128, 0)
-    natv[:, :, pl.ds(pl.multiple_of(edge, 8), 32), :] = jnp.zeros((DEPTHS, 4, 32, 128), jnp.int32)
-    for part in range(2):
-        place_rows(lambda y, rg: halo[part * 4 + y, pl.ds(rg * 8, 8), :], nat, part, edge, False)
-
-    for ref, parity in ((halo_vel, core), (halo_vel_other, 1 - core)):
+            vs = swap_blocks([halo[part * 4 + y, pl.ds(rg * 8, 8), :] for y in range(4)])
+            for v in range(4):
+                nat[part, v, pl.ds(rg * 8, 8), :] = vs[v]
+
+    natv[...] = jnp.zeros_like(natv)
+    for ref, parity in ((halo.at[pl.ds(8, 4)], core), (halo_vel_other, 1 - core)):
         for rg in range(4):
             vs = swap_blocks([ref[y, pl.ds(rg * 8, 8), :] for y in range(4)])
-            first_row = jnp.where(half == 0, 128, 8) + rg * 8
-            row0 = first_row if rg < 3 else jnp.where(half == 0, 128, 24)
-            depth = parity if rg < 3 else 2 + parity
+            if rg < 3:
+                row0, depth = jnp.where(half == 0, 0, 8) + rg * 8, parity
+            else:
+                row0, depth = jnp.where(half == 0, 0, 24), 2 + parity
             for v in range(4):
                 natv[depth, v, pl.ds(pl.multiple_of(row0, 8), 8), :] = vs[v].astype(jnp.int32)
 
     for part in range(2):
-        for i in range(BLK):
-            for v in range(4):
-                term[0, part, i, v] = nat[part, v, pl.ds(i, 8, stride=BLK), :]
+        for i in range(OWN):
+            for v in range(4):
+                term[0, part, i, v] = start[part, i, v]
+        for j in range(BLK - OWN):
+            for v in range(4):
+                term[0, part, OWN + j, v] = nat[part, v, pl.ds(j, 8, stride=4), :]
 
     def across(x):
         right = jnp.where(last, 0.0, pltpu.roll(x[0], 127, 1))
@@ -217,18 +264,53 @@
 
     def apply(part, source, finish):
         def row(i):
-            return [term[source, part, i, v] for v in range(4)]
-
-        h_low = [jnp.where(sub == 0, 0.0, pltpu.roll(h, 1, 0)) for h in across(row(BLK - 1))]
-        h_cur = across(row(0))
-        h_high = [jnp.where(sub == 7, 0.0, pltpu.roll(h, 7, 0)) for h in h_cur]
-        pair = [a + b for a, b in zip(h_low, h_cur)]
-        for i in range(BLK):
-            h_next = across(row(i + 1)) if i < BLK - 1 else h_high
-            pair_next = [a + b for a, b in zip(h_cur, h_next)]
-            for v in range(4):
-                finish(i, v, pair[v] + pair_next[v])
-            pair, h_cur = pair_next, h_next
+            return across([term[source, part, i, v] for v in range(4)])
+
+        down = {i: [pltpu.roll(h, 1, 0) for h in row(i)] for i in (OWN - 1, BLK - 1)}
+        h_own, h_halo = row(0), row(OWN)
+        up = {0: [pltpu.roll(h, 7, 0) for h in h_own], OWN: [pltpu.roll(h, 7, 0) for h in h_halo]}
+
+        def ends(at, other, flag, same):
+            return [
+                jnp.where(sub == at, flag * a, b) for a, b in zip(other, same)
+            ]
+
+        chains = (
+            (
+                range(OWN),
+                h_own,
+                ends(0, down[BLK - 1], before, down[OWN - 1]),
+                ends(7, up[OWN], after, up[0]),
+            ),
+            (
+                range(OWN, BLK),
+                h_halo,
+                ends(0, down[OWN - 1], after, down[BLK - 1]),
+                ends(7, up[0], before, up[OWN]),
+            ),
+        )
+        for span, h_cur, h_low, h_high in chains:
+            pair = [a + b for a, b in zip(h_low, h_cur)]
+            for i in span:
+                h_next = row(i + 1) if i < span[-1] else h_high
+                pair_next = [a + b for a, b in zip(h_cur, h_next)]
+                for v in range(4):
+                    finish(i, v, pair[v] + pair_next[v])
+                pair, h_cur = pair_next, h_next
+
+    def combine(i, v, coef):
+        real = imag = None
+        for k in range(TOP + 1):
+            c_re, c_im = coef(2 * k), coef(2 * k + 1)
+            t_re = term[k, 0, i, v]
+            t_im = term[k, 1, i, v]
+            re = c_re * t_re - c_im * t_im
+            im = c_re * t_im + c_im * t_re
+            real = re if real is None else real + re
+            imag = im if imag is None else imag + im
+        term[0, 0, i, v] = real
+        term[0, 1, i, v] = imag
+        return real
 
     @pl.loop(0, DEPTHS)
     def _(depth):
@@ -249,35 +331,40 @@
 
                 apply(part, k, next_term)
 
-        @pl.loop(0, BLK, unroll=10)
-        def _(i):
-            for v in range(4):
-                idx = natv[depth, v, pl.ds(i, 8, stride=BLK), :]
-                real = imag = None
-                for k in range(TOP + 1):
-                    c_re = gather_lanes(table[2 * k], idx)
-                    c_im = gather_lanes(table[2 * k + 1], idx)
-                    t_re = term[k, 0, i, v]
-                    t_im = term[k, 1, i, v]
-                    re = c_re * t_re - c_im * t_im
-                    im = c_re * t_im + c_im * t_re
-                    real = re if real is None else real + re
-                    imag = im if imag is None else imag + im
-                term[0, 0, i, v] = real
-                term[0, 1, i, v] = imag
-                img[v, pl.ds(i, 8, stride=BLK), :] = real
+        @pl.when(depth < AHEAD)
+        def _():
+            @pl.loop(0, OWN, unroll=4)
+            def _(i):
+                for v in range(4):
+                    img[v, pl.ds(i, 8, stride=PITCH), :] = combine(
+                        i, v, lambda n: coefs[depth, i, v, n]
+                    )
+
+        @pl.when(depth >= AHEAD)
+        def _():
+            @pl.loop(0, OWN, unroll=8)
+            def _(i):
+                for v in range(4):
+                    idx = index[depth - AHEAD, i, v]
+                    img[v, pl.ds(i, 8, stride=PITCH), :] = combine(
+                        i, v, lambda n: gather_lanes(table[n], idx)
+                    )
+
+        @pl.when(depth < DEPTHS - 1)
+        def _():
+            for j in range(BLK - OWN):
+                for v in range(4):
+                    idx = natv[depth, v, pl.ds(j, 8, stride=4), :]
+                    combine(OWN + j, v, lambda n: gather_lanes(table[n], idx))
 
         slot = jnp.where(depth % 2 == core, 0, 1)
         zl = depth // 2
 
         @pl.loop(0, 4, unroll=4)
         def _(n):
-            xq, zh = n // 2, n % 2
-            row0 = tile_row(xq, zh)
+            t = own_tile(half, n)
             for rg in range(4):
-                vals = swap_blocks(
-                    [img[v, pl.ds(pl.multiple_of(row0 + rg * 8, 8), 8), :] for v in range(4)]
-                )
+                vals = swap_blocks([img[v, tile_group(t, rg), :] for v in range(4)])
                 for y in range(4):
                     out[slot, (n * 2 + zl) * 4 + y, pl.ds(rg * 8, 8), :] = vals[y]
 
@@ -290,12 +377,12 @@
         in_specs=[vmem] * 6,
         out_specs=vmem,
         scratch_shapes=[
-            pltpu.VMEM((2, 4, ROWS, 128), jnp.float32),
-            pltpu.VMEM((DEPTHS, 4, ROWS, 128), jnp.int32),
+            pltpu.VMEM((2, 4, 32, 128), jnp.float32),
+            pltpu.VMEM((DEPTHS, 4, 32, 128), jnp.int32),
             pltpu.VMEM((TOP + 1, 2, BLK, 4, 8, 128), jnp.float32),
-            pltpu.VMEM((4, ROWS, 128), jnp.float32),
+            pltpu.VMEM((4, 8 * PITCH, 128), jnp.float32),
         ],
-        compiler_params=pltpu.CompilerParams(vmem_limit_bytes=40 * 1024 * 1024),
+        compiler_params=pltpu.CompilerParams(vmem_limit_bytes=28 * 1024 * 1024),
         cost_estimate=pl.CostEstimate(flops=70_000_000, bytes_accessed=4_000_000, transcendentals=0),
     )(*operands)
 
@@ -325,18 +412,22 @@
             ],
             axis=1,
         )
-        halo_vel = lax.ppermute(edge_vel, AXES, half_pairs())
-        halo = lax.ppermute(edge[:, 0], AXES, half_pairs())
+        halo = lax.ppermute(
+            jnp.concatenate([edge[:, 0], edge_vel], axis=0), AXES, half_pairs()
+        )
     with jax.named_scope("velocity"):
         vel_other = lax.ppermute(recv[:, 1], AXES, core_pairs())
-        halo_vel_other = lax.ppermute(halo_vel, AXES, core_pairs())
     with jax.named_scope("tables"):
         own = lax.dynamic_slice(coef_table, (freq, 0, 0, 0), (1, TOP + 1, 2, NV))
         own = own.reshape(COEFS, NV)
         table = jnp.pad(own[:, None], ((0, 0), (0, 0), (0, 128 - NV)))
         table = jnp.broadcast_to(table, (COEFS, 8, 128))
+    with jax.named_scope("prepare"):
+        start, index, coefs, zero = prepare(recv, vel_other, table)
+    with jax.named_scope("velocity"):
+        halo_vel_other = lax.ppermute(halo[8:] + zero[:1], AXES, core_pairs())
     with jax.named_scope("extrapolate"):
-        out = extrapolate(recv, halo, halo_vel, vel_other, halo_vel_other, table)
+        out = extrapolate(start, index, coefs, halo, halo_vel_other, table)
     with jax.named_scope("image"):
         total = out[0] + lax.ppermute(out[1], AXES, core_pairs())
         parts = lax.all_to_all(total, AXES, 0, 0, axis_index_groups=groups_of_half())

time: 74.2 us -> 71.4 us (0.962)
  waiting for transfers between devices: 24.3 us -> 19.2 us
  Pallas kernels: 20.4 us -> 22.9 us
  starting transfers between devices: 12.9 us -> 12.1 us
    pallas_call x0 -> x1, Pallas kernels: none -> 6.32 us  [prepare(): pl.pallas_call(prepare_kernel, out_shape=(jax.ShapeDtypeStruct((2, OWN, 4...]
    ppermute x3 -> x2, waiting for transfers between devices: 5.93 us -> 1.13 us  [the longest x1 1.08 us: per_device(): halo_vel_other = lax.ppermute(halo[8:] + zero[:1], AXES, core_pairs())]
    pallas_call x1, Pallas kernels: 17 us -> 13.5 us  [extrapolate(): pl.pallas_call(kernel, out_shape=jax.ShapeDtypeStruct((2, 32, 32, 128), j...]
    ppermute x3 -> x2, starting transfers between devices: 3.4 us -> 2.43 us  [the longest x1 2.18 us: per_device(): lax.ppermute(jnp.concatenate([edge[:, 0], edge_vel], axis=0), AXES, half_...]
  transfers between devices with their start and end apart: 6 -> 5, of which waited for: 4 -> 4; matrix products, arithmetic and copies ran while one was open for 0% -> 0% of each run, Pallas kernels for 0% -> 9%
where the time goes in v3:
time: 71.4 us; the launch traced here: 71.1 us
  Pallas kernels  22.9 us (32%)
  waiting for transfers between devices  19.2 us (27%)
  blocking collectives  16.3 us (23%)
  starting transfers between devices  12.1 us (17%)
    all_to_all x1, waiting for transfers between devices, per_device(): recv = lax.all_to_all(send, AXES, 0, 0, axis_index_groups=groups_of_half())  16.4 us
    all_to_all x1, blocking collectives, per_device(): lax.all_to_all(total, AXES, 0, 0, axis_index_groups=groups_of_half())  16.3 us
    pallas_call x1, Pallas kernels, extrapolate(): pl.pallas_call(kernel, out_shape=jax.ShapeDtypeStruct((2, 32, 32, 128), j...  13.5 us
    all_to_all x1, starting transfers between devices, per_device(): recv = lax.all_to_all(send, AXES, 0, 0, axis_index_groups=groups_of_half())  9.36 us
    pallas_call x1, Pallas kernels, prepare(): pl.pallas_call(prepare_kernel, out_shape=(jax.ShapeDtypeStruct((2, OWN, 4...  6.32 us
    pallas_call x1, Pallas kernels, pack(): pl.pallas_call(pack_kernel, out_shape=jax.ShapeDtypeStruct((32, 2, 32, 12...  2.4 us
    ppermute x1, starting transfers between devices, per_device(): lax.ppermute(jnp.concatenate([edge[:, 0], edge_vel], axis=0), AXES, half_...  2.18 us
    ppermute x1, waiting for transfers between devices, per_device(): total = out[0] + lax.ppermute(out[1], AXES, core_pairs())  1.73 us
  transfers between devices with their start and end apart: 5, of which 4 were waited for; matrix products, arithmetic and copies ran while one was open for 0% of the time, Pallas kernels for 9%

profile of v3, /device:TPU:0, one launch (start us, length us, event | category | flops | bytes accessed | tf_op | source)
XLA Modules:
  0.0 71.1 jit_solution(8901812483072416461)
XLA Ops:
  0.0 0.0 copy-start
  0.0 2.4 %pack.1 = f32[32,2,32,128]{3,2,1,0:T(8,128)} custom-call(f32[64,2,32,128]{3,2,1,0:T(8,128)} %surface.1, s32[1,32,128]{2,1,0:T(8,128)} %vel.1), custom_call_target="tpu_custom_call" | custom-call | tf_op jit(solution)/shard_map/pack/pallas_call | solution.py:118
  2.4 9.4 %all-to-all-start = ((f32[32,2,32,128]{3,2,1,0:T(8,128)}), f32[32,2,32,128]{3,2,1,0:T(8,128)S(1)}, u32[]{:S(2)}, u32[]{:S(2)}) async-start(f32[32,2,32,128]{3,2,1,0:T(8,128)} %pack.1), calls=%async_computation | async-start | bytes 2097152 | tf_op jit(solution)/shard_map/spread/all_to_all | solution.py:403
  11.9 0.0 copy-done
  11.9 16.4 %all-to-all-done.recv = f32[32,2,32,128]{3,2,1,0:T(8,128)S(1)} async-done(((f32[32,2,32,128]{3,2,1,0:T(8,128)}), f32[32,2,32,128]{3,2,1,0:T(8,128)S(1)}, u32[]{:S(2)}, u32[]{:S(2)}) %all-to-all-start) | async-done | bytes 1048608 | tf_op jit(solution)/shard_map/spread/all_to_all | solution.py:403
  28.3 0.1 collective-permute-start
  28.6 2.2 %collective-permute-start.1 = (f32[12,32,128]{2,1,0:T(8,128)S(1)}, f32[12,32,128]{2,1,0:T(8,128)S(1)}, u32[]{:S(2)}, u32[]{:S(2)}) collective-permute-start(f32[12,32,128]{2,1,0:T(8,128)S(1)} %maximum_maximum_fusion), channel_id=1, source_target_pairs={{0,24},{32,56},{64,88},{96,120},{4,28},{36,60},{68,92},{100,124},{... | collective-permute-start | bytes 589832 | tf_op jit(solution)/shard_map/halo/ppermute | solution.py:415
  30.7 0.0 collective-permute-done.vel_other
  30.8 6.3 %prepare.1 = (f32[2,16,4,8,128]{4,3,2,1,0:T(8,128)S(1)}, s32[1,16,4,8,128]{4,3,2,1,0:T(8,128)S(1)}, f32[3,16,4,18,8,128]{5,4,3,2,1,0:T(8,128)S(1)}, f32[8,128]{1,0:T(8,128)S(1)}) custom-call(f32[32,2,32,128]{3,2,1,0:T(8,128)S(1)} %all-to-all-done.recv, f32[32,32,128]{2,1,0:T(8,128)S(1)} %collective-permute-done.vel_other, ...), custom_call_target="tpu_custom_call" | custom-call | flops 20000000 | bytes 4000000 | tf_op jit(solution)/shard_map/prepare/pallas_call | solution.py:205
  37.1 0.1 collective-permute-done.1.halo
  37.2 0.3 collective-permute-start.2
  37.4 1.1 %collective-permute-done.2.halo_vel_other = f32[4,32,128]{2,1,0:T(8,128)S(1)} collective-permute-done((f32[4,32,128]{2,1,0:T(8,128)S(1)}, f32[4,32,128]{2,1,0:T(8,128)S(1)}, u32[]{:S(2)}, u32[]{:S(2)}) %collective-permute-start.2) | collective-permute-done | bytes 65568 | tf_op jit(solution)/shard_map/velocity/ppermute | solution.py:428
  38.5 13.5 %extrapolate.1 = f32[2,32,32,128]{3,2,1,0:T(8,128)S(1)} custom-call(f32[2,16,4,8,128]{4,3,2,1,0:T(8,128)S(1)} %get-tuple-element.9.start, s32[1,16,4,8,128]{4,3,2,1,0:T(8,128)S(1)} %get-tuple-element.10.index, f32[3,16,4,18,8,128]{5,4,3,2,1,0:T(8,128)S(1)} %get-tuple-element.11.coefs, f32[12,32,128]{2,1,0:T(8,128)S(1)} %collective-permute-done.1.halo, ...), custom_call_target="tpu_custom_call" | custom-call | flops 70000000 | bytes 4000000 | tf_op jit(solution)/shard_map/extrapolate/pallas_call | solution.py:374
  52.0 0.3 collective-permute-start.3
  52.3 1.7 %collective-permute-done.3 = f32[32,32,128]{2,1,0:T(8,128)S(1)} collective-permute-done((f32[32,32,128]{2,1,0:T(8,128)S(1)}, f32[32,32,128]{2,1,0:T(8,128)S(1)}, u32[]{:S(2)}, u32[]{:S(2)}) %collective-permute-start.3) | collective-permute-done | bytes 524320 | tf_op jit(solution)/shard_map/image/ppermute | solution.py:432
  54.0 0.1 fusion
  54.1 16.3 %all_to_all.10.parts = f32[32,32,128]{2,1,0:T(8,128)S(1)} all-to-all(f32[32,32,128]{2,1,0:T(8,128)S(1)} %fusion), channel_id=1, replica_groups={{0,1,2,3,64,65,66,67,4,5,6,7,68,69,70,71,8,9,10,11,72,73,74,75,12,13,14..., dimensions={0} | all-to-all | bytes 1048576 | tf_op jit(solution)/shard_map/image/all_to_all | solution.py:433
  70.4 0.7 %image.1 = f32[1,32,128]{2,1,0:T(8,128)} custom-call(f32[32,32,128]{2,1,0:T(8,128)S(1)} %all_to_all.10.parts), custom_call_target="tpu_custom_call" | custom-call | tf_op jit(solution)/shard_map/image/pallas_call | solution.py:144
  (13 shorter events, 0.2 us)
Async XLA Ops:
  0.0 11.9 %copy-start = (f32[64,9,2,64]{3,2,1,0:T(2,128)S(1)}, f32[64,9,2,64]{3,2,1,0:T(2,128)}, u32[]{:S(2)}) copy-start(f32[64,9,2,64]{3,2,1,0:T(2,128)} %param.4) | copy-start | bytes 884740
  2.4 25.9 %all-to-all-start = ((f32[32,2,32,128]{3,2,1,0:T(8,128)}), f32[32,2,32,128]{3,2,1,0:T(8,128)S(1)}, u32[]{:S(2)}, u32[]{:S(2)}) async-start(f32[32,2,32,128]{3,2,1,0:T(8,128)} %pack.1), calls=%async_computation | async-start | bytes 2097152 | tf_op jit(solution)/shard_map/spread/all_to_all | solution.py:403
  28.3 2.4 %collective-permute-start = (f32[32,32,128]{2,1,0:T(8,128)S(1)}, f32[32,32,128]{2,1,0:T(8,128)S(1)}, u32[]{:S(2)}, u32[]{:S(2)}) collective-permute-start(f32[32,32,128]{2,1,0:T(8,128)S(1)} %slice_bitcast_fusion.2), channel_id=1, source_target_pairs={{0,32},{32,0},{64,96},{96,64},{4,36},{36,4},{68,100},{100,68},{1,3... | collective-permute-start | bytes 1572872 | tf_op jit(solution)/shard_map/velocity/ppermute | solution.py:419
  28.6 8.6 %collective-permute-start.1 = (f32[12,32,128]{2,1,0:T(8,128)S(1)}, f32[12,32,128]{2,1,0:T(8,128)S(1)}, u32[]{:S(2)}, u32[]{:S(2)}) collective-permute-start(f32[12,32,128]{2,1,0:T(8,128)S(1)} %maximum_maximum_fusion), channel_id=1, source_target_pairs={{0,24},{32,56},{64,88},{96,120},{4,28},{36,60},{68,92},{100,124},{... | collective-permute-start | bytes 589832 | tf_op jit(solution)/shard_map/halo/ppermute | solution.py:415
  37.2 1.3 %collective-permute-start.2 = (f32[4,32,128]{2,1,0:T(8,128)S(1)}, f32[4,32,128]{2,1,0:T(8,128)S(1)}, u32[]{:S(2)}, u32[]{:S(2)}) collective-permute-start(f32[4,32,128]{2,1,0:T(8,128)S(1)} %slice_add_fusion), channel_id=1, source_target_pairs={{0,32},{32,0},{64,96},{96,64},{4,36},{36,4},{68,100},{100,68},{1,3... | collective-permute-start | bytes 196616 | tf_op jit(solution)/shard_map/velocity/ppermute | solution.py:428
  52.0 2.0 %collective-permute-start.3 = (f32[32,32,128]{2,1,0:T(8,128)S(1)}, f32[32,32,128]{2,1,0:T(8,128)S(1)}, u32[]{:S(2)}, u32[]{:S(2)}) collective-permute-start(f32[32,32,128]{2,1,0:T(8,128)S(1)} %slice_bitcast_fusion), channel_id=1, source_target_pairs={{0,32},{32,0},{64,96},{96,64},{4,36},{36,4},{68,100},{100,68},{1,3... | collective-permute-start | bytes 1572872 | tf_op jit(solution)/shard_map/image/ppermute | solution.py:432

commit v4 on v3

v4 whole, which is shorter than its diff:
```python
import jax
import jax.numpy as jnp
from jax import lax
from jax.experimental import pallas as pl
from jax.experimental.pallas import tpu as pltpu
from jax.sharding import PartitionSpec as P

AXES = ("sec", "gx", "gy")
OWN = 16
BLK = 20
PITCH = 24
WAYS = 5
AHEAD = 3
TOP = 8
DEPTHS = 4
NV = 64
COEFS = 2 * (TOP + 1)


def flat(x, y, zh, zl, core):
    return ((zl * 2 + core) * 8 + x * 2 + zh) * 4 + y


def from_rim(half, q):
    return q if half == 0 else 3 - q


def groups_of_quadrant():
    return [
        [
            flat(from_rim(half_x, xq), from_rim(half_y, yq), zh, zl, core)
            for xq in range(2)
            for zh in range(2)
            for zl in range(2)
            for yq in range(2)
        ]
        for half_x in range(2)
        for half_y in range(2)
        for core in range(2)
    ]


def pairs(partner):
    return [
        (flat(x, y, zh, zl, core), flat(*partner(x, y, zh, zl, core)))
        for x in range(4)
        for y in range(4)
        for zh in range(2)
        for zl in range(2)
        for core in range(2)
    ]


def core_pairs():
    return pairs(lambda x, y, zh, zl, core: (x, y, zh, zl, 1 - core))


def gather_lanes(x, idx):
    return jnp.take_along_axis(x, idx, axis=1, mode="promise_in_bounds")


def lanes():
    return lax.broadcasted_iota(jnp.int32, (8, 128), 1)


def rows(rg):
    return pl.ds(rg * 8, 8)


def turn(x, by):
    return pltpu.roll(x, by, 1)


def swap_blocks(x):
    lane = lanes()
    low = lane < 64
    even = (lane // 32) % 2 == 0
    near = [jnp.where(low, x[i], turn(x[i + 2], 64)) for i in range(2)]
    far = [jnp.where(low, turn(x[i], 64), x[i + 2]) for i in range(2)]
    res = []
    for a, b in (near, far):
        res.append(jnp.where(even, a, turn(b, 32)))
        res.append(jnp.where(even, turn(a, 96), b))
    return res


def coordinates():
    sec, gx, y = lax.axis_index("sec"), lax.axis_index("gx"), lax.axis_index("gy")
    x, zh = gx // 2, gx % 2
    return x, y, zh, sec // 2, sec % 2


def pack_kernel(surface, vel, send, buf, vel_buf, sems):
    _, y, _, zl, core = coordinates()
    lane = lanes()
    idx = 4 * (lane % 32) + lane // 32
    idx = jnp.where(y < 2, idx, 127 - idx)
    vel_copy = pltpu.make_async_copy(vel, vel_buf, sems.at[4])
    vel_copy.start()
    copies = [
        pltpu.make_async_copy(
            surface.at[pl.ds(core * 16 + j * 4, 4), zl], buf.at[pl.ds(j * 4, 4)], sems.at[j]
        )
        for j in range(4)
    ]
    for copy in copies:
        copy.start()
    vel_copy.wait()
    for rg in range(4):
        value = gather_lanes(vel_buf[0, rows(rg), :].astype(jnp.float32), idx)
        for n in range(16):
            send[n, 2, rows(rg), :] = value
    for j, copy in enumerate(copies):
        copy.wait()
        for n in range(j * 4, j * 4 + 4):
            for part in range(2):
                for rg in range(4):
                    send[n, part, rows(rg), :] = gather_lanes(buf[n, part, rows(rg), :], idx)


def pack(surface, vel):
    vmem = pl.BlockSpec(memory_space=pltpu.VMEM)
    return pl.pallas_call(
        pack_kernel,
        out_shape=jax.ShapeDtypeStruct((16, 3, 32, 128), jnp.float32),
        in_specs=[pl.BlockSpec(memory_space=pl.ANY)] * 2,
        out_specs=vmem,
        scratch_shapes=[
            pltpu.VMEM((16, 2, 32, 128), jnp.float32),
            pltpu.VMEM((1, 32, 128), jnp.int32),
            pltpu.SemaphoreType.DMA((5,)),
        ],
        compiler_params=pltpu.CompilerParams(vmem_limit_bytes=60 * 1024 * 1024),
    )(surface.reshape(32, 2, 2, 32, 128), vel)


def sum_kernel(parts, image):
    y = lax.axis_index("gy")
    lane = lanes()
    column = jnp.where(y < 2, lane, 127 - lane)
    idx = 32 * (column % 4) + column // 4
    for rg in range(4):
        terms = [parts[n, rows(rg), :] for n in range(16)]
        while len(terms) > 1:
            terms = [a + b for a, b in zip(terms[::2], terms[1::2])]
        image[0, rows(rg), :] = gather_lanes(terms[0], idx)


def add_up(parts):
    vmem = pl.BlockSpec(memory_space=pltpu.VMEM)
    return pl.pallas_call(
        sum_kernel,
        out_shape=jax.ShapeDtypeStruct((1, 32, 128), jnp.float32),
        in_specs=[vmem],
        out_specs=vmem,
        compiler_params=pltpu.CompilerParams(vmem_limit_bytes=16 * 1024 * 1024),
    )(parts)


def own_tile(half, n):
    return jnp.where(half == 0, n, (n + 2) % 4)


def edge_kernel(recv, own, below, beside, corner, table):
    x, _, _, _, _ = coordinates()
    half = x // 2
    lane = lanes()
    inner = lane % 32
    block = lane // 32
    last = 32 * (inner % 4) + 24 + inner // 4
    edge = 2 + (1 - half)
    for k in range(TOP + 1):
        pair = jnp.concatenate([own[0, k], own[1, k]], axis=1)
        for r in range(2):
            table[2 * k + r] = jnp.broadcast_to(pair[r : r + 1], (8, 128))

    for yq in range(2):
        for rg in range(4):
            for f in range(2):
                for part in range(2):
                    below[(f * 2 + part) * 2 + yq, rows(rg), :] = recv[
                        (edge * 2 + f) * 2 + yq, part, rows(rg), :
                    ]
            if rg < 3:
                zl, row0 = 0, 8 * (1 - half) + rg * 8
            else:
                zl, row0 = 1, 24 * (1 - half)
            below[8 + yq, rows(rg), :] = recv[
                (edge * 2 + zl) * 2 + yq, 2, pl.ds(pl.multiple_of(row0, 8), 8), :
            ]

    def final_columns(n, f, slab, rg):
        return gather_lanes(recv[(n * 2 + f) * 2 + 1, slab, rows(rg), :], last)

    for rg in range(4):
        for slab in range(3):
            a, b = [final_columns(edge, f, slab, rg) for f in range(2)]
            corner[slab, rows(rg), :] = jnp.where(lane < 64, a, b)
            for t in range(2):
                near, far = own_tile(half, t), own_tile(half, t + 2)
                a, b, c, d = [
                    final_columns(n, f, slab, rg) for f in range(2) for n in (far, near)
                ]
                beside[slab, pl.ds(t * 32 + rg * 8, 8), :] = jnp.where(
                    block < 2, jnp.where(block == 0, a, b), jnp.where(block == 2, c, d)
                )


def edges(recv, own):
    vmem = pl.BlockSpec(memory_space=pltpu.VMEM)
    return pl.pallas_call(
        edge_kernel,
        out_shape=(
            jax.ShapeDtypeStruct((10, 32, 128), jnp.float32),
            jax.ShapeDtypeStruct((3, 64, 128), jnp.float32),
            jax.ShapeDtypeStruct((3, 32, 128), jnp.float32),
            jax.ShapeDtypeStruct((COEFS, 8, 128), jnp.float32),
        ),
        in_specs=[vmem] * 2,
        out_specs=(vmem,) * 4,
        compiler_params=pltpu.CompilerParams(vmem_limit_bytes=16 * 1024 * 1024),
    )(recv, own)


def edge_velocity_kernel(below, beside, corner, zero, vel):
    for rg in range(4):
        for q in range(2):
            vel[q, rows(rg), :] = below[8 + q, rows(rg), :] + zero[...]
            vel[2 + q, rows(rg), :] = beside[2, pl.ds(q * 32 + rg * 8, 8), :]
        vel[4, rows(rg), :] = corner[2, rows(rg), :]


def edge_velocity(*operands):
    vmem = pl.BlockSpec(memory_space=pltpu.VMEM)
    return pl.pallas_call(
        edge_velocity_kernel,
        out_shape=jax.ShapeDtypeStruct((5, 32, 128), jnp.float32),
        in_specs=[vmem] * 4,
        out_specs=vmem,
        compiler_params=pltpu.CompilerParams(vmem_limit_bytes=16 * 1024 * 1024),
    )(*operands)


def tile_group(t, rg):
    return pl.ds(pl.multiple_of((2 * t + rg // 2) * PITCH + 8 * (rg % 2), 8), 8)


def prepare_kernel(recv, vel_other, table, start, index, coefs, zero, nat, natv):
    x, _, _, _, core = coordinates()
    zero[...] = jnp.zeros_like(zero)
    half = x // 2
    shift = jnp.where(lanes() < 64, 0, NV)

    @pl.loop(0, 4)
    def _(n):
        t = own_tile(half, n)
        for rg in range(4):
            dst = tile_group(t, rg)
            for part in range(2):
                vs = swap_blocks([recv[n * 4 + m, part, rows(rg), :] for m in range(4)])
                for v in range(4):
                    nat[part, v, dst, :] = vs[v]
            for zl in range(2):
                for mine in range(2):
                    two = [
                        recv[n * 4 + zl * 2 + yq, 2, rows(rg), :]
                        if mine
                        else vel_other[n * 4 + zl * 2 + yq, rows(rg), :]
                        for yq in range(2)
                    ]
                    depth = zl * 2 + (core if mine else 1 - core)
                    vs = swap_blocks(two + two)
                    for v in range(4):
                        natv[depth, v, dst, :] = vs[v].astype(jnp.int32) + shift

    def block(i):
        return pl.ds(i, 8, stride=PITCH)

    for i in range(OWN):
        for v in range(4):
            for part in range(2):
                start[part, i, v] = nat[part, v, block(i), :]
            for depth in range(AHEAD, DEPTHS):
                index[depth - AHEAD, i, v] = natv[depth, v, block(i), :]

    @pl.loop(0, AHEAD)
    def _(depth):
        @pl.loop(0, OWN, unroll=16)
        def _(i):
            for v in range(4):
                idx = natv[depth, v, block(i), :]
                for n in range(COEFS):
                    coefs[depth, i, v, n] = gather_lanes(table[n], idx)


def prepare(recv, vel_other, table):
    vmem = pl.BlockSpec(memory_space=pltpu.VMEM)
    return pl.pallas_call(
        prepare_kernel,
        out_shape=(
            jax.ShapeDtypeStruct((2, OWN, 4, 8, 128), jnp.float32),
            jax.ShapeDtypeStruct((DEPTHS - AHEAD, OWN, 4, 8, 128), jnp.int32),
            jax.ShapeDtypeStruct((AHEAD, OWN, 4, COEFS, 8, 128), jnp.float32),
            jax.ShapeDtypeStruct((8, 128), jnp.float32),
        ),
        in_specs=[vmem] * 3,
        out_specs=(vmem,) * 4,
        scratch_shapes=[
            pltpu.VMEM((2, 4, 8 * PITCH, 128), jnp.float32),
            pltpu.VMEM((DEPTHS, 4, 8 * PITCH, 128), jnp.int32),
        ],
        compiler_params=pltpu.CompilerParams(vmem_limit_bytes=24 * 1024 * 1024),
        cost_estimate=pl.CostEstimate(flops=20_000_000, bytes_accessed=4_000_000, transcendentals=0),
    )(recv, vel_other, table)


def kernel(
    start, index, coefs, below, beside, corner, vel_other, table, out,
    nat, natv, side, sidev, term, img
):
    x, _, _, _, core = coordinates()
    half = x // 2
    lane = lanes()
    sub = lax.broadcasted_iota(jnp.int32, (8, 128), 0)
    first = lane % 64 == 0
    last = lane % 64 == 63
    low = lane < 64
    shift = jnp.where(low, 0, NV)
    before = jnp.where(half == 0, 0.0, 1.0)
    after = 1.0 - before

    def block(i):
        return pl.ds(i, 8, stride=PITCH)

    for part in range(2):
        for rg in range(4):
            vs = swap_blocks(
                [below[(f * 2 + part) * 2 + yq, rows(rg), :] for f in range(2) for yq in range(2)]
            )
            for v in range(4):
                nat[part, v, rows(rg), :] = vs[v]
            nat[part, 4, rows(rg), :] = corner[part, rows(rg), :]

    def both(value, zl):
        other = turn(value, 64)
        return (jnp.where(low, value, other) if zl == 0 else jnp.where(low, other, value)).astype(
            jnp.int32
        ) + shift

    natv[...] = jnp.zeros_like(natv)
    for mine in range(2):
        parity = core if mine else 1 - core
        for rg in range(4):
            two = [below[8 + yq, rows(rg), :] if mine else vel_other[yq, rows(rg), :] for yq in range(2)]
            vs = swap_blocks(two + two)
            if rg < 3:
                row0, depth = jnp.where(half == 0, 0, 8) + rg * 8, parity
            else:
                row0, depth = jnp.where(half == 0, 0, 24), 2 + parity
            for v in range(4):
                natv[depth, v, pl.ds(pl.multiple_of(row0, 8), 8), :] = (
                    vs[v].astype(jnp.int32) + shift
                )
            value = corner[2, rows(rg), :] if mine else vel_other[4, rows(rg), :]
            for zl in range(2):
                natv[2 * zl + parity, 4, rows(rg), :] = both(value, zl)

    for t in range(4):
        for rg in range(4):
            dst = tile_group(t, rg)
            src = pl.ds((t % 2) * 32 + rg * 8, 8)

            def placed(value):
                return value if t < 2 else turn(value, 32)

            for part in range(2):
                side[part, dst, :] = placed(beside[part, src, :])
            for mine in range(2):
                parity = core if mine else 1 - core
                value = placed(beside[2, src, :] if mine else vel_other[2 + t % 2, rows(rg), :])
                for zl in range(2):
                    sidev[2 * zl + parity, dst, :] = both(value, zl)

    for part in range(2):
        for i in range(OWN):
            for v in range(4):
                term[0, part, i, v] = start[part, i, v]
            term[0, part, i, 4] = side[part, block(i), :]
        for j in range(BLK - OWN):
            for v in range(WAYS):
                term[0, part, OWN + j, v] = nat[part, v, pl.ds(j, 8, stride=4), :]

    def across(x):
        right = jnp.where(last, x[4], turn(x[0], 127))
        left = jnp.where(first, 0.0, turn(x[3], 1))
        back = jnp.where(last, x[3], turn(x[4], 127))
        q = [x[0] + x[1], x[1] + x[2], x[2] + x[3]]
        return [
            (left + x[0]) + q[0],
            q[0] + q[1],
            q[1] + q[2],
            q[2] + (x[3] + right),
            (back + x[4]) + (x[4] + turn(x[4], 1)),
        ]

    def apply(part, source, finish):
        def row(i):
            return across([term[source, part, i, v] for v in range(WAYS)])

        down = {i: [pltpu.roll(h, 1, 0) for h in row(i)] for i in (OWN - 1, BLK - 1)}
        h_own, h_halo = row(0), row(OWN)
        up = {0: [pltpu.roll(h, 7, 0) for h in h_own], OWN: [pltpu.roll(h, 7, 0) for h in h_halo]}

        def ends(at, other, flag, same):
            return [
                jnp.where(sub == at, flag * a, b) for a, b in zip(other, same)
            ]

        chains = (
            (
                range(OWN),
                h_own,
                ends(0, down[BLK - 1], before, down[OWN - 1]),
                ends(7, up[OWN], after, up[0]),
            ),
            (
                range(OWN, BLK),
                h_halo,
                ends(0, down[OWN - 1], after, down[BLK - 1]),
                ends(7, up[0], before, up[OWN]),
            ),
        )
        for span, h_cur, h_low, h_high in chains:
            pair = [a + b for a, b in zip(h_low, h_cur)]
            for i in span:
                h_next = row(i + 1) if i < span[-1] else h_high
                pair_next = [a + b for a, b in zip(h_cur, h_next)]
                for v in range(WAYS):
                    finish(i, v, pair[v] + pair_next[v])
                pair, h_cur = pair_next, h_next

    def combine(i, v, coef):
        real = imag = None
        for k in range(TOP + 1):
            c_re, c_im = coef(2 * k), coef(2 * k + 1)
            t_re = term[k, 0, i, v]
            t_im = term[k, 1, i, v]
            re = c_re * t_re - c_im * t_im
            im = c_re * t_im + c_im * t_re
            real = re if real is None else real + re
            imag = im if imag is None else imag + im
        term[0, 0, i, v] = real
        term[0, 1, i, v] = imag
        return real

    @pl.loop(0, DEPTHS)
    def _(depth):
        for part in range(2):

            def first_term(i, v, s):
                term[1, part, i, v] = 0.125 * s - term[0, part, i, v]

            apply(part, 0, first_term)

        @pl.loop(1, TOP)
        def _(k):
            for part in range(2):

                def next_term(i, v, s):
                    cur = term[k, part, i, v]
                    term[k + 1, part, i, v] = (0.25 * s - cur) - (cur + term[k - 1, part, i, v])

                apply(part, k, next_term)

        @pl.when(depth < AHEAD)
        def _():
            @pl.loop(0, OWN, unroll=16)
            def _(i):
                for v in range(4):
                    img[v, pl.ds(i, 8, stride=PITCH), :] = combine(
                        i, v, lambda n: coefs[depth, i, v, n]
                    )

        @pl.when(depth >= AHEAD)
        def _():
            @pl.loop(0, OWN, unroll=8)
            def _(i):
                for v in range(4):
                    idx = index[depth - AHEAD, i, v]
                    img[v, pl.ds(i, 8, stride=PITCH), :] = combine(
                        i, v, lambda n: gather_lanes(table[n], idx)
                    )

        @pl.when(depth < DEPTHS - 1)
        def _():
            for j in range(BLK - OWN):
                for v in range(WAYS):
                    idx = natv[depth, v, pl.ds(j, 8, stride=4), :]
                    combine(OWN + j, v, lambda n: gather_lanes(table[n], idx))
            for i in range(OWN):
                idx = sidev[depth, block(i), :]
                combine(i, 4, lambda n: gather_lanes(table[n], idx))

        slot = jnp.where(depth % 2 == core, 0, 1)
        zl = depth // 2

        @pl.loop(0, 4, unroll=4)
        def _(n):
            t = own_tile(half, n)
            even = (lane // 32) % 2 == 0
            for rg in range(4):
                vals = [img[v, tile_group(t, rg), :] for v in range(4)]
                vals = [a + turn(a, 64) for a in vals]
                a, b = [jnp.where(low, vals[i], vals[i + 2]) for i in range(2)]
                out[slot, (n * 2 + zl) * 2, rows(rg), :] = jnp.where(even, a, turn(b, 32))
                out[slot, (n * 2 + zl) * 2 + 1, rows(rg), :] = jnp.where(even, turn(a, 96), b)


def extrapolate(*operands):
    vmem = pl.BlockSpec(memory_space=pltpu.VMEM)
    return pl.pallas_call(
        kernel,
        out_shape=jax.ShapeDtypeStruct((2, 16, 32, 128), jnp.float32),
        in_specs=[vmem] * 8,
        out_specs=vmem,
        scratch_shapes=[
            pltpu.VMEM((2, WAYS, 32, 128), jnp.float32),
            pltpu.VMEM((DEPTHS, WAYS, 32, 128), jnp.int32),
            pltpu.VMEM((2, 8 * PITCH, 128), jnp.float32),
            pltpu.VMEM((DEPTHS, 8 * PITCH, 128), jnp.int32),
            pltpu.VMEM((TOP + 1, 2, BLK, WAYS, 8, 128), jnp.float32),
            pltpu.VMEM((4, 8 * PITCH, 128), jnp.float32),
        ],
        compiler_params=pltpu.CompilerParams(vmem_limit_bytes=28 * 1024 * 1024),
        cost_estimate=pl.CostEstimate(flops=70_000_000, bytes_accessed=4_000_000, transcendentals=0),
    )(*operands)


def per_device(surface, coef_table, vel_index):
    groups = groups_of_quadrant()

    with jax.named_scope("pack"):
        send = pack(surface, vel_index)
    with jax.named_scope("tables"):
        x, y, zh, zl, core = coordinates()
        xq = jnp.where(x < 2, x, 3 - x)
        yq = jnp.where(y < 2, y, 3 - y)
        freq = core * 32 + (((xq * 2 + zh) * 2 + zl) * 2 + yq) * 2
        own = lax.dynamic_slice(coef_table, (freq, 0, 0, 0), (2, TOP + 1, 2, NV))
    with jax.named_scope("spread"):
        recv = lax.all_to_all(send, AXES, 0, 0, axis_index_groups=groups)
    with jax.named_scope("halo"):
        below, beside, corner, table = edges(recv, own)
        below = lax.ppermute(below, AXES, pairs(lambda x, y, *rest: (3 - x, y, *rest)))
        beside = lax.ppermute(beside, AXES, pairs(lambda x, y, *rest: (x, 3 - y, *rest)))
        corner = lax.ppermute(corner, AXES, pairs(lambda x, y, *rest: (3 - x, 3 - y, *rest)))
    with jax.named_scope("velocity"):
        vel_other = lax.ppermute(recv[:, 2], AXES, core_pairs())
    with jax.named_scope("prepare"):
        start, index, coefs, zero = prepare(recv, vel_other, table)
    with jax.named_scope("velocity"):
        edge_vel = lax.ppermute(edge_velocity(below, beside, corner, zero), AXES, core_pairs())
    with jax.named_scope("extrapolate"):
        out = extrapolate(start, index, coefs, below, beside, corner, edge_vel, table)
    with jax.named_scope("image"):
        total = out[0] + lax.ppermute(out[1], AXES, core_pairs())
        parts = lax.all_to_all(total, AXES, 0, 0, axis_index_groups=groups)
        return add_up(parts)


def solution(mesh):
    in_specs = (P(None, None, "gx", "gy"), P(), P("sec", "gx", "gy"))
    out_specs = P("sec", "gx", "gy")
    return jax.shard_map(
        per_device, mesh=mesh, in_specs=in_specs, out_specs=out_specs, check_vma=False
    )
```

time: 71.4 us -> 69.2 us (0.969)
  Pallas kernels: 22.9 us -> 27.7 us
  blocking collectives: 16.3 us -> 11.7 us
  waiting for transfers between devices: 19.2 us -> 15.4 us
  starting transfers between devices: 12.1 us -> 13.8 us
    all_to_all x1, blocking collectives: 16.3 us -> 11.7 us  [per_device(): parts = lax.all_to_all(total, AXES, 0, 0, axis_index_groups=groups)]
    pallas_call x2 -> x4, Pallas kernels: 15.9 us -> 20.3 us  [the longest x1 17.7 us: extrapolate(): pl.pallas_call(kernel, out_shape=jax.ShapeDtypeStruct((2, 16, 32, 128), j...]
    ppermute x3 -> x5, starting transfers between devices: 2.51 us -> 6.16 us  [the longest x1 2.18 us: per_device(): lax.ppermute(beside, AXES, pairs(lambda x, y, *rest: (x, 3 - y, *rest)))]
    all_to_all x1, waiting for transfers between devices: 16.4 us -> 12.8 us  [per_device(): recv = lax.all_to_all(send, AXES, 0, 0, axis_index_groups=groups)]
    all_to_all x1, starting transfers between devices: 9.36 us -> 7.45 us  [per_device(): recv = lax.all_to_all(send, AXES, 0, 0, axis_index_groups=groups)]
  transfers between devices with their start and end apart: 5 -> 7, of which waited for: 4 -> 3; matrix products, arithmetic and copies ran while one was open for 0% -> 0% of each run, Pallas kernels for 9% -> 10%
where the time goes in v4:
time: 69.2 us; the launch traced here: 68.9 us
  Pallas kernels  27.7 us (40%)
  waiting for transfers between devices  15.4 us (22%)
  starting transfers between devices  13.8 us (20%)
  blocking collectives  11.7 us (17%)
    pallas_call x1, Pallas kernels, extrapolate(): pl.pallas_call(kernel, out_shape=jax.ShapeDtypeStruct((2, 16, 32, 128), j...  17.7 us
    all_to_all x1, waiting for transfers between devices, per_device(): recv = lax.all_to_all(send, AXES, 0, 0, axis_index_groups=groups)  12.8 us
    all_to_all x1, blocking collectives, per_device(): parts = lax.all_to_all(total, AXES, 0, 0, axis_index_groups=groups)  11.7 us
    all_to_all x1, starting transfers between devices, per_device(): recv = lax.all_to_all(send, AXES, 0, 0, axis_index_groups=groups)  7.45 us
    pallas_call x1, Pallas kernels, prepare(): pl.pallas_call(prepare_kernel, out_shape=(jax.ShapeDtypeStruct((2, OWN, 4...  6.76 us
    pallas_call x1, Pallas kernels, pack(): pl.pallas_call(pack_kernel, out_shape=jax.ShapeDtypeStruct((16, 3, 32, 12...  2.31 us
    ppermute x1, starting transfers between devices, per_device(): lax.ppermute(beside, AXES, pairs(lambda x, y, *rest: (x, 3 - y, *rest)))  2.18 us
    ppermute x1, starting transfers between devices, per_device(): lax.ppermute(below, AXES, pairs(lambda x, y, *rest: (3 - x, y, *rest)))  2.18 us
  transfers between devices with their start and end apart: 7, of which 3 were waited for; matrix products, arithmetic and copies ran while one was open for 0% of the time, Pallas kernels for 10%

profile of v4, /device:TPU:0, one launch (start us, length us, event | category | flops | bytes accessed | tf_op | source)
XLA Modules:
  0.0 68.9 jit_solution(16280135702517258498)
XLA Ops:
  0.0 0.0 copy-start
  0.0 2.3 %pack.1 = f32[16,3,32,128]{3,2,1,0:T(8,128)} custom-call(f32[32,2,2,32,128]{4,3,2,1,0:T(8,128)} %bitcast.11, s32[1,32,128]{2,1,0:T(8,128)} %vel.1), custom_call_target="tpu_custom_call" | custom-call | tf_op jit(solution)/shard_map/pack/pallas_call | solution.py:123
  2.3 7.5 %all-to-all-start = ((f32[16,3,32,128]{3,2,1,0:T(8,128)}), f32[16,3,32,128]{3,2,1,0:T(8,128)S(1)}, u32[]{:S(2)}, u32[]{:S(2)}) async-start(f32[16,3,32,128]{3,2,1,0:T(8,128)} %pack.1), calls=%async_computation | async-start | bytes 1572864 | tf_op jit(solution)/shard_map/spread/all_to_all | solution.py:551
  9.8 12.8 %all-to-all-done.recv = f32[16,3,32,128]{3,2,1,0:T(8,128)S(1)} async-done(((f32[16,3,32,128]{3,2,1,0:T(8,128)}), f32[16,3,32,128]{3,2,1,0:T(8,128)S(1)}, u32[]{:S(2)}, u32[]{:S(2)}) %all-to-all-start) | async-done | bytes 786464 | tf_op jit(solution)/shard_map/spread/all_to_all | solution.py:551
  22.6 0.1 collective-permute-start
  22.7 0.0 copy-done
  22.8 0.2 halo.1
  23.0 2.2 %collective-permute-start.1 = (f32[10,32,128]{2,1,0:T(8,128)S(1)}, f32[10,32,128]{2,1,0:T(8,128)S(1)}, u32[]{:S(2)}, u32[]{:S(2)}) collective-permute-start(f32[10,32,128]{2,1,0:T(8,128)S(1)} %get-tuple-element.17), channel_id=1, source_target_pairs={{0,24},{32,56},{64,88},{96,120},{4,28},{36,60},{68,92},{100,124},{... | collective-permute-start | bytes 491528 | tf_op jit(solution)/shard_map/halo/ppermute | solution.py:554
  25.2 2.2 %collective-permute-start.2 = (f32[3,64,128]{2,1,0:T(8,128)S(1)}, f32[3,64,128]{2,1,0:T(8,128)S(1)}, u32[]{:S(2)}, u32[]{:S(2)}) collective-permute-start(f32[3,64,128]{2,1,0:T(8,128)S(1)} %get-tuple-element.18), channel_id=1, source_target_pairs={{0,3},{32,35},{64,67},{96,99},{4,7},{36,39},{68,71},{100,103},{1,2... | collective-permute-start | bytes 294920 | tf_op jit(solution)/shard_map/halo/ppermute | solution.py:555
  27.4 1.6 %collective-permute-start.3 = (f32[3,32,128]{2,1,0:T(8,128)S(1)}, f32[3,32,128]{2,1,0:T(8,128)S(1)}, u32[]{:S(2)}, u32[]{:S(2)}) collective-permute-start(f32[3,32,128]{2,1,0:T(8,128)S(1)} %get-tuple-element.19), channel_id=1, source_target_pairs={{0,27},{32,59},{64,91},{96,123},{4,31},{36,63},{68,95},{100,127},{... | collective-permute-start | bytes 147464 | tf_op jit(solution)/shard_map/halo/ppermute | solution.py:556
  29.0 0.0 collective-permute-done.vel_other
  29.0 6.8 %prepare.1 = (f32[2,16,4,8,128]{4,3,2,1,0:T(8,128)S(1)}, s32[1,16,4,8,128]{4,3,2,1,0:T(8,128)S(1)}, f32[3,16,4,18,8,128]{5,4,3,2,1,0:T(8,128)S(1)}, f32[8,128]{1,0:T(8,128)S(1)}) custom-call(f32[16,3,32,128]{3,2,1,0:T(8,128)S(1)} %all-to-all-done.recv, f32[16,32,128]{2,1,0:T(8,128)S(1)} %collective-permute-done.vel_other, ...), custom_call_target="tpu_custom_call" | custom-call | flops 20000000 | bytes 4000000 | tf_op jit(solution)/shard_map/prepare/pallas_call | solution.py:298
  35.8 0.0 collective-permute-done.3.corner
  35.8 0.0 collective-permute-done.2.beside
  35.8 0.0 collective-permute-done.1.below
  35.8 0.1 collective-permute-start.4
  35.9 1.3 %collective-permute-done.4.vel_other = f32[5,32,128]{2,1,0:T(8,128)S(1)} collective-permute-done((f32[5,32,128]{2,1,0:T(8,128)S(1)}, f32[5,32,128]{2,1,0:T(8,128)S(1)}, u32[]{:S(2)}, u32[]{:S(2)}) %collective-permute-start.4) | collective-permute-done | bytes 81952 | tf_op jit(solution)/shard_map/velocity/ppermute | solution.py:562
  37.2 17.7 %extrapolate.1 = f32[2,16,32,128]{3,2,1,0:T(8,128)S(1)} custom-call(f32[2,16,4,8,128]{4,3,2,1,0:T(8,128)S(1)} %get-tuple-element.14.start, s32[1,16,4,8,128]{4,3,2,1,0:T(8,128)S(1)} %get-tuple-element.15.index, f32[3,16,4,18,8,128]{5,4,3,2,1,0:T(8,128)S(1)} %get-tuple-element.16.coefs, f32[10,32,128]{2,1,0:T(8,128)S(1)} %collective-permute-done.1.below, ...), custom_call_target="tpu_custom_call" | custom-call | flops 70000000 | bytes 4000000 | tf_op jit(solution)/shard_map/extrapolate/pallas_call | solution.py:521
  54.9 0.2 collective-permute-start.5
  55.2 1.4 %collective-permute-done.5 = f32[16,32,128]{2,1,0:T(8,128)S(1)} collective-permute-done((f32[16,32,128]{2,1,0:T(8,128)S(1)}, f32[16,32,128]{2,1,0:T(8,128)S(1)}, u32[]{:S(2)}, u32[]{:S(2)}) %collective-permute-start.5) | collective-permute-done | bytes 262176 | tf_op jit(solution)/shard_map/image/ppermute | solution.py:566
  56.6 11.7 %all_to_all.10.parts = f32[16,32,128]{2,1,0:T(8,128)S(1)} all-to-all(f32[16,32,128]{2,1,0:T(8,128)S(1)} %fusion), channel_id=1, replica_groups={{0,1,64,65,4,5,68,69,8,9,72,73,12,13,76,77},{32,33,96,97,36,37,100,101,..., dimensions={0} | all-to-all | bytes 524288 | tf_op jit(solution)/shard_map/image/all_to_all | solution.py:567
  68.2 0.7 %image.1 = f32[1,32,128]{2,1,0:T(8,128)} custom-call(f32[16,32,128]{2,1,0:T(8,128)S(1)} %all_to_all.10.parts), custom_call_target="tpu_custom_call" | custom-call | tf_op jit(solution)/shard_map/image/pallas_call | solution.py:151
  (5 shorter events, 0.1 us)
Async XLA Ops:
  0.0 22.7 %copy-start = (f32[64,9,2,64]{3,2,1,0:T(2,128)S(1)}, f32[64,9,2,64]{3,2,1,0:T(2,128)}, u32[]{:S(2)}) copy-start(f32[64,9,2,64]{3,2,1,0:T(2,128)} %param.4) | copy-start | bytes 884740
  2.3 20.3 %all-to-all-start = ((f32[16,3,32,128]{3,2,1,0:T(8,128)}), f32[16,3,32,128]{3,2,1,0:T(8,128)S(1)}, u32[]{:S(2)}, u32[]{:S(2)}) async-start(f32[16,3,32,128]{3,2,1,0:T(8,128)} %pack.1), calls=%async_computation | async-start | bytes 1572864 | tf_op jit(solution)/shard_map/spread/all_to_all | solution.py:551
  22.6 6.3 %collective-permute-start = (f32[16,32,128]{2,1,0:T(8,128)S(1)}, f32[16,32,128]{2,1,0:T(8,128)S(1)}, u32[]{:S(2)}, u32[]{:S(2)}) collective-permute-start(f32[16,32,128]{2,1,0:T(8,128)S(1)} %slice_bitcast_fusion.2), channel_id=1, source_target_pairs={{0,32},{32,0},{64,96},{96,64},{4,36},{36,4},{68,100},{100,68},{1,3... | collective-permute-start | bytes 786440 | tf_op jit(solution)/shard_map/velocity/ppermute | solution.py:558
  23.0 12.8 %collective-permute-start.1 = (f32[10,32,128]{2,1,0:T(8,128)S(1)}, f32[10,32,128]{2,1,0:T(8,128)S(1)}, u32[]{:S(2)}, u32[]{:S(2)}) collective-permute-start(f32[10,32,128]{2,1,0:T(8,128)S(1)} %get-tuple-element.17), channel_id=1, source_target_pairs={{0,24},{32,56},{64,88},{96,120},{4,28},{36,60},{68,92},{100,124},{... | collective-permute-start | bytes 491528 | tf_op jit(solution)/shard_map/halo/ppermute | solution.py:554
  25.2 10.6 %collective-permute-start.2 = (f32[3,64,128]{2,1,0:T(8,128)S(1)}, f32[3,64,128]{2,1,0:T(8,128)S(1)}, u32[]{:S(2)}, u32[]{:S(2)}) collective-permute-start(f32[3,64,128]{2,1,0:T(8,128)S(1)} %get-tuple-element.18), channel_id=1, source_target_pairs={{0,3},{32,35},{64,67},{96,99},{4,7},{36,39},{68,71},{100,103},{1,2... | collective-permute-start | bytes 294920 | tf_op jit(solution)/shard_map/halo/ppermute | solution.py:555
  27.4 8.4 %collective-permute-start.3 = (f32[3,32,128]{2,1,0:T(8,128)S(1)}, f32[3,32,128]{2,1,0:T(8,128)S(1)}, u32[]{:S(2)}, u32[]{:S(2)}) collective-permute-start(f32[3,32,128]{2,1,0:T(8,128)S(1)} %get-tuple-element.19), channel_id=1, source_target_pairs={{0,27},{32,59},{64,91},{96,123},{4,31},{36,63},{68,95},{100,127},{... | collective-permute-start | bytes 147464 | tf_op jit(solution)/shard_map/halo/ppermute | solution.py:556
  35.8 1.4 %collective-permute-start.4 = (f32[5,32,128]{2,1,0:T(8,128)S(1)}, f32[5,32,128]{2,1,0:T(8,128)S(1)}, u32[]{:S(2)}, u32[]{:S(2)}) collective-permute-start(f32[5,32,128]{2,1,0:T(8,128)S(1)} %velocity.1), channel_id=1, source_target_pairs={{0,32},{32,0},{64,96},{96,64},{4,36},{36,4},{68,100},{100,68},{1,3... | collective-permute-start | bytes 245768 | tf_op jit(solution)/shard_map/velocity/ppermute | solution.py:562
  54.9 1.6 %collective-permute-start.5 = (f32[16,32,128]{2,1,0:T(8,128)S(1)}, f32[16,32,128]{2,1,0:T(8,128)S(1)}, u32[]{:S(2)}, u32[]{:S(2)}) collective-permute-start(f32[16,32,128]{2,1,0:T(8,128)S(1)} %slice_bitcast_fusion), channel_id=1, source_target_pairs={{0,32},{32,0},{64,96},{96,64},{4,36},{36,4},{68,100},{100,68},{1,3... | collective-permute-start | bytes 786440 | tf_op jit(solution)/shard_map/image/ppermute | solution.py:566

commit v5 on v4

--- a/solution.py
+++ b/solution.py
@@ -309,14 +309,37 @@
             pltpu.VMEM((2, 4, 8 * PITCH, 128), jnp.float32),
             pltpu.VMEM((DEPTHS, 4, 8 * PITCH, 128), jnp.int32),
         ],
-        compiler_params=pltpu.CompilerParams(vmem_limit_bytes=24 * 1024 * 1024),
+        compiler_params=pltpu.CompilerParams(vmem_limit_bytes=8 * 1024 * 1024),
         cost_estimate=pl.CostEstimate(flops=20_000_000, bytes_accessed=4_000_000, transcendentals=0),
     )(recv, vel_other, table)
 
 
+def late_kernel(index, table, coefs):
+    for depth in range(DEPTHS - AHEAD):
+
+        @pl.loop(0, OWN, unroll=16)
+        def _(i):
+            for v in range(4):
+                idx = index[depth, i, v]
+                for n in range(COEFS):
+                    coefs[depth, i, v, n] = gather_lanes(table[n], idx)
+
+
+def late(index, table):
+    vmem = pl.BlockSpec(memory_space=pltpu.VMEM)
+    return pl.pallas_call(
+        late_kernel,
+        out_shape=jax.ShapeDtypeStruct((DEPTHS - AHEAD, OWN, 4, COEFS, 8, 128), jnp.float32),
+        in_specs=[vmem] * 2,
+        out_specs=vmem,
+        compiler_params=pltpu.CompilerParams(vmem_limit_bytes=8 * 1024 * 1024),
+        cost_estimate=pl.CostEstimate(flops=5_000_000, bytes_accessed=1_000_000, transcendentals=0),
+    )(index, table)
+
+
 def kernel(
-    start, index, coefs, below, beside, corner, vel_other, table, out,
-    nat, natv, side, sidev, term, img
+    start, late_coefs, coefs, below, beside, corner, vel_other, table, out,
+    nat, natv, side, sidev, term, pair_sum, img
 ):
     x, _, _, _, core = coordinates()
     half = x // 2
@@ -326,8 +349,7 @@
     last = lane % 64 == 63
     low = lane < 64
     shift = jnp.where(low, 0, NV)
-    before = jnp.where(half == 0, 0.0, 1.0)
-    after = 1.0 - before
+    rim = {0: (sub == 0) & (half == 0), 7: (sub == 7) & (half == 1)}
 
     def block(i):
         return pl.ds(i, 8, stride=PITCH)
@@ -407,33 +429,37 @@
         def row(i):
             return across([term[source, part, i, v] for v in range(WAYS)])
 
-        down = {i: [pltpu.roll(h, 1, 0) for h in row(i)] for i in (OWN - 1, BLK - 1)}
-        h_own, h_halo = row(0), row(OWN)
-        up = {0: [pltpu.roll(h, 7, 0) for h in h_own], OWN: [pltpu.roll(h, 7, 0) for h in h_halo]}
-
-        def ends(at, other, flag, same):
-            return [
-                jnp.where(sub == at, flag * a, b) for a, b in zip(other, same)
-            ]
+        known = {i: row(i) for i in (0, OWN - 1, OWN, BLK - 1)}
+        down = {i: [pltpu.roll(h, 1, 0) for h in known[i]] for i in (OWN - 1, BLK - 1)}
+        up = {i: [pltpu.roll(h, 7, 0) for h in known[i]] for i in (0, OWN)}
+
+        def ends(at, other, same):
+            return [jnp.where(sub == at, a, b) for a, b in zip(other, same)]
+
+        def open_ends(at, other, same):
+            return [jnp.where(rim[at], 0.0, a) for a in ends(at, other, same)]
 
         chains = (
             (
                 range(OWN),
-                h_own,
-                ends(0, down[BLK - 1], before, down[OWN - 1]),
-                ends(7, up[OWN], after, up[0]),
+                known[0],
+                open_ends(0, down[BLK - 1], down[OWN - 1]),
+                open_ends(7, up[OWN], up[0]),
             ),
             (
                 range(OWN, BLK),
-                h_halo,
-                ends(0, down[OWN - 1], after, down[BLK - 1]),
-                ends(7, up[0], before, up[OWN]),
+                known[OWN],
+                ends(0, down[OWN - 1], down[BLK - 1]),
+                ends(7, up[0], up[OWN]),
             ),
         )
         for span, h_cur, h_low, h_high in chains:
             pair = [a + b for a, b in zip(h_low, h_cur)]
             for i in span:
-                h_next = row(i + 1) if i < span[-1] else h_high
+                if i == span[-1]:
+                    h_next = h_high
+                else:
+                    h_next = known[i + 1] if i + 1 in known else row(i + 1)
                 pair_next = [a + b for a, b in zip(h_cur, h_next)]
                 for v in range(WAYS):
                     finish(i, v, pair[v] + pair_next[v])
@@ -458,38 +484,38 @@
         for part in range(2):
 
             def first_term(i, v, s):
-                term[1, part, i, v] = 0.125 * s - term[0, part, i, v]
+                new = 0.125 * s
+                pair_sum[part, i, v] = new
+                term[1, part, i, v] = new - term[0, part, i, v]
 
             apply(part, 0, first_term)
 
-        @pl.loop(1, TOP)
+        @pl.loop(1, TOP, unroll=TOP - 1)
         def _(k):
             for part in range(2):
 
                 def next_term(i, v, s):
-                    cur = term[k, part, i, v]
-                    term[k + 1, part, i, v] = (0.25 * s - cur) - (cur + term[k - 1, part, i, v])
+                    new = 0.25 * s - pair_sum[part, i, v]
+                    pair_sum[part, i, v] = new
+                    term[k + 1, part, i, v] = new - term[k, part, i, v]
 
                 apply(part, k, next_term)
 
-        @pl.when(depth < AHEAD)
-        def _():
+        def combine_own(ref, step):
             @pl.loop(0, OWN, unroll=16)
             def _(i):
                 for v in range(4):
                     img[v, pl.ds(i, 8, stride=PITCH), :] = combine(
-                        i, v, lambda n: coefs[depth, i, v, n]
+                        i, v, lambda n: ref[step, i, v, n]
                     )
+
+        @pl.when(depth < AHEAD)
+        def _():
+            combine_own(coefs, depth)
 
         @pl.when(depth >= AHEAD)
         def _():
-            @pl.loop(0, OWN, unroll=8)
-            def _(i):
-                for v in range(4):
-                    idx = index[depth - AHEAD, i, v]
-                    img[v, pl.ds(i, 8, stride=PITCH), :] = combine(
-                        i, v, lambda n: gather_lanes(table[n], idx)
-                    )
+            combine_own(late_coefs, depth - AHEAD)
 
         @pl.when(depth < DEPTHS - 1)
         def _():
@@ -529,9 +555,10 @@
             pltpu.VMEM((2, 8 * PITCH, 128), jnp.float32),
             pltpu.VMEM((DEPTHS, 8 * PITCH, 128), jnp.int32),
             pltpu.VMEM((TOP + 1, 2, BLK, WAYS, 8, 128), jnp.float32),
+            pltpu.VMEM((2, BLK, WAYS, 8, 128), jnp.float32),
             pltpu.VMEM((4, 8 * PITCH, 128), jnp.float32),
         ],
-        compiler_params=pltpu.CompilerParams(vmem_limit_bytes=28 * 1024 * 1024),
+        compiler_params=pltpu.CompilerParams(vmem_limit_bytes=14 * 1024 * 1024),
         cost_estimate=pl.CostEstimate(flops=70_000_000, bytes_accessed=4_000_000, transcendentals=0),
     )(*operands)
 
@@ -560,8 +587,10 @@
         start, index, coefs, zero = prepare(recv, vel_other, table)
     with jax.named_scope("velocity"):
         edge_vel = lax.ppermute(edge_velocity(below, beside, corner, zero), AXES, core_pairs())
+    with jax.named_scope("late"):
+        late_coefs = late(index, table)
     with jax.named_scope("extrapolate"):
-        out = extrapolate(start, index, coefs, below, beside, corner, edge_vel, table)
+        out = extrapolate(start, late_coefs, coefs, below, beside, corner, edge_vel, table)
     with jax.named_scope("image"):
         total = out[0] + lax.ppermute(out[1], AXES, core_pairs())
         parts = lax.all_to_all(total, AXES, 0, 0, axis_index_groups=groups)

time: 69.2 us -> 67.8 us (0.980)
  waiting for transfers between devices: 15.4 us -> 14 us
    pallas_call x1, Pallas kernels: 17.7 us -> 15.7 us  [extrapolate(): pl.pallas_call(kernel, out_shape=jax.ShapeDtypeStruct((2, 16, 32, 128), j...]
    pallas_call x0 -> x1, Pallas kernels: none -> 1.48 us  [late(): pl.pallas_call(late_kernel, out_shape=jax.ShapeDtypeStruct((DEPTHS - AHEA...]
    ppermute x1, waiting for transfers between devices: 1.26 us -> 0.01 us  [per_device(): lax.ppermute(edge_velocity(below, beside, corner, zero), AXES, core_pairs())]
  transfers between devices with their start and end apart: 7 -> 7, of which waited for: 3 -> 2; matrix products, arithmetic and copies ran while one was open for 0% -> 0% of each run, Pallas kernels for 10% -> 13%
where the time goes in v5:
time: 67.8 us; the launch traced here: 67.5 us
  Pallas kernels  27.2 us (40%)
  starting transfers between devices  14.2 us (21%)
  waiting for transfers between devices  14 us (21%)
  blocking collectives  11.9 us (18%)
    pallas_call x1, Pallas kernels, extrapolate(): pl.pallas_call(kernel, out_shape=jax.ShapeDtypeStruct((2, 16, 32, 128), j...  15.7 us
    all_to_all x1, waiting for transfers between devices, per_device(): recv = lax.all_to_all(send, AXES, 0, 0, axis_index_groups=groups)  12.8 us
    all_to_all x1, blocking collectives, per_device(): parts = lax.all_to_all(total, AXES, 0, 0, axis_index_groups=groups)  11.9 us
    all_to_all x1, starting transfers between devices, per_device(): recv = lax.all_to_all(send, AXES, 0, 0, axis_index_groups=groups)  7.45 us
    pallas_call x1, Pallas kernels, prepare(): pl.pallas_call(prepare_kernel, out_shape=(jax.ShapeDtypeStruct((2, OWN, 4...  6.76 us
    pallas_call x1, Pallas kernels, pack(): pl.pallas_call(pack_kernel, out_shape=jax.ShapeDtypeStruct((16, 3, 32, 12...  2.31 us
    ppermute x1, starting transfers between devices, per_device(): lax.ppermute(beside, AXES, pairs(lambda x, y, *rest: (x, 3 - y, *rest)))  2.18 us
    ppermute x1, starting transfers between devices, per_device(): lax.ppermute(below, AXES, pairs(lambda x, y, *rest: (3 - x, y, *rest)))  2.18 us
  transfers between devices with their start and end apart: 7, of which 2 were waited for; matrix products, arithmetic and copies ran while one was open for 0% of the time, Pallas kernels for 13%

profile of v5, /device:TPU:0, one launch (start us, length us, event | category | flops | bytes accessed | tf_op | source)
XLA Modules:
  0.0 67.5 jit_solution(1338231417869608776)
XLA Ops:
  0.0 0.0 copy-start
  0.0 2.3 %pack.1 = f32[16,3,32,128]{3,2,1,0:T(8,128)} custom-call(f32[32,2,2,32,128]{4,3,2,1,0:T(8,128)} %bitcast.11, s32[1,32,128]{2,1,0:T(8,128)} %vel.1), custom_call_target="tpu_custom_call" | custom-call | tf_op jit(solution)/shard_map/pack/pallas_call | solution.py:123
  2.3 7.5 %all-to-all-start = ((f32[16,3,32,128]{3,2,1,0:T(8,128)}), f32[16,3,32,128]{3,2,1,0:T(8,128)S(1)}, u32[]{:S(2)}, u32[]{:S(2)}) async-start(f32[16,3,32,128]{3,2,1,0:T(8,128)} %pack.1), calls=%async_computation | async-start | bytes 1572864 | tf_op jit(solution)/shard_map/spread/all_to_all | solution.py:578
  9.8 12.8 %all-to-all-done.recv = f32[16,3,32,128]{3,2,1,0:T(8,128)S(1)} async-done(((f32[16,3,32,128]{3,2,1,0:T(8,128)}), f32[16,3,32,128]{3,2,1,0:T(8,128)S(1)}, u32[]{:S(2)}, u32[]{:S(2)}) %all-to-all-start) | async-done | bytes 786464 | tf_op jit(solution)/shard_map/spread/all_to_all | solution.py:578
  22.6 0.1 collective-permute-start
  22.7 0.0 copy-done
  22.8 0.2 halo.1
  23.0 2.2 %collective-permute-start.1 = (f32[10,32,128]{2,1,0:T(8,128)S(1)}, f32[10,32,128]{2,1,0:T(8,128)S(1)}, u32[]{:S(2)}, u32[]{:S(2)}) collective-permute-start(f32[10,32,128]{2,1,0:T(8,128)S(1)} %get-tuple-element.17), channel_id=1, source_target_pairs={{0,24},{32,56},{64,88},{96,120},{4,28},{36,60},{68,92},{100,124},{... | collective-permute-start | bytes 491528 | tf_op jit(solution)/shard_map/halo/ppermute | solution.py:581
  25.2 2.2 %collective-permute-start.2 = (f32[3,64,128]{2,1,0:T(8,128)S(1)}, f32[3,64,128]{2,1,0:T(8,128)S(1)}, u32[]{:S(2)}, u32[]{:S(2)}) collective-permute-start(f32[3,64,128]{2,1,0:T(8,128)S(1)} %get-tuple-element.18), channel_id=1, source_target_pairs={{0,3},{32,35},{64,67},{96,99},{4,7},{36,39},{68,71},{100,103},{1,2... | collective-permute-start | bytes 294920 | tf_op jit(solution)/shard_map/halo/ppermute | solution.py:582
  27.4 1.6 %collective-permute-start.3 = (f32[3,32,128]{2,1,0:T(8,128)S(1)}, f32[3,32,128]{2,1,0:T(8,128)S(1)}, u32[]{:S(2)}, u32[]{:S(2)}) collective-permute-start(f32[3,32,128]{2,1,0:T(8,128)S(1)} %get-tuple-element.19), channel_id=1, source_target_pairs={{0,27},{32,59},{64,91},{96,123},{4,31},{36,63},{68,95},{100,127},{... | collective-permute-start | bytes 147464 | tf_op jit(solution)/shard_map/halo/ppermute | solution.py:583
  29.0 0.0 collective-permute-done.vel_other
  29.0 6.8 %prepare.1 = (f32[2,16,4,8,128]{4,3,2,1,0:T(8,128)S(1)}, s32[1,16,4,8,128]{4,3,2,1,0:T(8,128)S(1)}, f32[3,16,4,18,8,128]{5,4,3,2,1,0:T(8,128)S(1)}, f32[8,128]{1,0:T(8,128)S(1)}) custom-call(f32[16,3,32,128]{3,2,1,0:T(8,128)S(1)} %all-to-all-done.recv, f32[16,32,128]{2,1,0:T(8,128)S(1)} %collective-permute-done.vel_other, ...), custom_call_target="tpu_custom_call" | custom-call | flops 20000000 | bytes 4000000 | tf_op jit(solution)/shard_map/prepare/pallas_call | solution.py:298
  35.8 0.0 collective-permute-done.3.corner
  35.8 0.0 collective-permute-done.2.beside
  35.8 0.0 collective-permute-done.1.below
  35.8 0.1 collective-permute-start.4
  35.9 1.5 %late.1.late_coefs = f32[1,16,4,18,8,128]{5,4,3,2,1,0:T(8,128)S(1)} custom-call(s32[1,16,4,8,128]{4,3,2,1,0:T(8,128)S(1)} %get-tuple-element.15.index, f32[18,8,128]{2,1,0:T(8,128)S(1)} %get-tuple-element.13.table), custom_call_target="tpu_custom_call" | custom-call | flops 5000000 | bytes 1000000 | tf_op jit(solution)/shard_map/late/pallas_call | solution.py:330
  37.4 0.0 collective-permute-done.4.vel_other
  37.4 15.7 %extrapolate.1 = f32[2,16,32,128]{3,2,1,0:T(8,128)S(1)} custom-call(f32[2,16,4,8,128]{4,3,2,1,0:T(8,128)S(1)} %get-tuple-element.14.start, f32[1,16,4,18,8,128]{5,4,3,2,1,0:T(8,128)S(1)} %late.1.late_coefs, f32[3,16,4,18,8,128]{5,4,3,2,1,0:T(8,128)S(1)} %get-tuple-element.16.coefs, f32[10,32,128]{2,1,0:T(8,128)S(1)} %collective-permute-done.1.below, ...), custom_call_target="tpu_custom_call" | custom-call | flops 70000000 | bytes 4000000 | tf_op jit(solution)/shard_map/extrapolate/pallas_call | solution.py:547
  53.2 0.6 collective-permute-start.5
  53.7 1.2 %collective-permute-done.5 = f32[16,32,128]{2,1,0:T(8,128)S(1)} collective-permute-done((f32[16,32,128]{2,1,0:T(8,128)S(1)}, f32[16,32,128]{2,1,0:T(8,128)S(1)}, u32[]{:S(2)}, u32[]{:S(2)}) %collective-permute-start.5) | collective-permute-done | bytes 262176 | tf_op jit(solution)/shard_map/image/ppermute | solution.py:595
  54.9 11.9 %all_to_all.10.parts = f32[16,32,128]{2,1,0:T(8,128)S(1)} all-to-all(f32[16,32,128]{2,1,0:T(8,128)S(1)} %fusion), channel_id=1, replica_groups={{0,1,64,65,4,5,68,69,8,9,72,73,12,13,76,77},{32,33,96,97,36,37,100,101,..., dimensions={0} | all-to-all | bytes 524288 | tf_op jit(solution)/shard_map/image/all_to_all | solution.py:596
  66.8 0.7 %image.1 = f32[1,32,128]{2,1,0:T(8,128)} custom-call(f32[16,32,128]{2,1,0:T(8,128)S(1)} %all_to_all.10.parts), custom_call_target="tpu_custom_call" | custom-call | tf_op jit(solution)/shard_map/image/pallas_call | solution.py:151
  (5 shorter events, 0.1 us)
Async XLA Ops:
  0.0 22.7 %copy-start = (f32[64,9,2,64]{3,2,1,0:T(2,128)S(1)}, f32[64,9,2,64]{3,2,1,0:T(2,128)}, u32[]{:S(2)}) copy-start(f32[64,9,2,64]{3,2,1,0:T(2,128)} %param.4) | copy-start | bytes 884740
  2.3 20.3 %all-to-all-start = ((f32[16,3,32,128]{3,2,1,0:T(8,128)}), f32[16,3,32,128]{3,2,1,0:T(8,128)S(1)}, u32[]{:S(2)}, u32[]{:S(2)}) async-start(f32[16,3,32,128]{3,2,1,0:T(8,128)} %pack.1), calls=%async_computation | async-start | bytes 1572864 | tf_op jit(solution)/shard_map/spread/all_to_all | solution.py:578
  22.6 6.3 %collective-permute-start = (f32[16,32,128]{2,1,0:T(8,128)S(1)}, f32[16,32,128]{2,1,0:T(8,128)S(1)}, u32[]{:S(2)}, u32[]{:S(2)}) collective-permute-start(f32[16,32,128]{2,1,0:T(8,128)S(1)} %slice_bitcast_fusion.2), channel_id=1, source_target_pairs={{0,32},{32,0},{64,96},{96,64},{4,36},{36,4},{68,100},{100,68},{1,3... | collective-permute-start | bytes 786440 | tf_op jit(solution)/shard_map/velocity/ppermute | solution.py:585
  23.0 12.8 %collective-permute-start.1 = (f32[10,32,128]{2,1,0:T(8,128)S(1)}, f32[10,32,128]{2,1,0:T(8,128)S(1)}, u32[]{:S(2)}, u32[]{:S(2)}) collective-permute-start(f32[10,32,128]{2,1,0:T(8,128)S(1)} %get-tuple-element.17), channel_id=1, source_target_pairs={{0,24},{32,56},{64,88},{96,120},{4,28},{36,60},{68,92},{100,124},{... | collective-permute-start | bytes 491528 | tf_op jit(solution)/shard_map/halo/ppermute | solution.py:581
  25.2 10.6 %collective-permute-start.2 = (f32[3,64,128]{2,1,0:T(8,128)S(1)}, f32[3,64,128]{2,1,0:T(8,128)S(1)}, u32[]{:S(2)}, u32[]{:S(2)}) collective-permute-start(f32[3,64,128]{2,1,0:T(8,128)S(1)} %get-tuple-element.18), channel_id=1, source_target_pairs={{0,3},{32,35},{64,67},{96,99},{4,7},{36,39},{68,71},{100,103},{1,2... | collective-permute-start | bytes 294920 | tf_op jit(solution)/shard_map/halo/ppermute | solution.py:582
  27.4 8.4 %collective-permute-start.3 = (f32[3,32,128]{2,1,0:T(8,128)S(1)}, f32[3,32,128]{2,1,0:T(8,128)S(1)}, u32[]{:S(2)}, u32[]{:S(2)}) collective-permute-start(f32[3,32,128]{2,1,0:T(8,128)S(1)} %get-tuple-element.19), channel_id=1, source_target_pairs={{0,27},{32,59},{64,91},{96,123},{4,31},{36,63},{68,95},{100,127},{... | collective-permute-start | bytes 147464 | tf_op jit(solution)/shard_map/halo/ppermute | solution.py:583
  35.8 1.6 %collective-permute-start.4 = (f32[5,32,128]{2,1,0:T(8,128)S(1)}, f32[5,32,128]{2,1,0:T(8,128)S(1)}, u32[]{:S(2)}, u32[]{:S(2)}) collective-permute-start(f32[5,32,128]{2,1,0:T(8,128)S(1)} %velocity.1), channel_id=1, source_target_pairs={{0,32},{32,0},{64,96},{96,64},{4,36},{36,4},{68,100},{100,68},{1,3... | collective-permute-start | bytes 245768 | tf_op jit(solution)/shard_map/velocity/ppermute | solution.py:589
  53.2 1.7 %collective-permute-start.5 = (f32[16,32,128]{2,1,0:T(8,128)S(1)}, f32[16,32,128]{2,1,0:T(8,128)S(1)}, u32[]{:S(2)}, u32[]{:S(2)}) collective-permute-start(f32[16,32,128]{2,1,0:T(8,128)S(1)} %slice_bitcast_fusion), channel_id=1, source_target_pairs={{0,32},{32,0},{64,96},{96,64},{4,36},{36,4},{68,100},{100,68},{1,3... | collective-permute-start | bytes 786440 | tf_op jit(solution)/shard_map/image/ppermute | solution.py:595

commit v6 on v5

--- a/solution.py
+++ b/solution.py
@@ -15,6 +15,7 @@
 DEPTHS = 4
 NV = 64
 COEFS = 2 * (TOP + 1)
+BY_ROW = 6
 
 
 def flat(x, y, zh, zl, core):
@@ -57,6 +58,25 @@
 
 def gather_lanes(x, idx):
     return jnp.take_along_axis(x, idx, axis=1, mode="promise_in_bounds")
+
+
+def gather_rows(x, idx):
+    return jnp.take_along_axis(x, idx, axis=0, mode="promise_in_bounds")
+
+
+def look_up(indices, table, row_table, store):
+    low = [idx & 7 for idx in indices]
+    bits = [[(idx & (8 << b)) == 0 for b in range(3)] for idx in indices]
+    for v, idx in enumerate(indices):
+        for n in range(BY_ROW, COEFS):
+            store(v, n, gather_lanes(table[n], idx))
+    for n in range(BY_ROW):
+        entries = [row_table[n, j] for j in range(8)]
+        for v in range(len(indices)):
+            level = [gather_rows(e, low[v]) for e in entries]
+            for bit in bits[v]:
+                level = [jnp.where(bit, a, b) for a, b in zip(level[::2], level[1::2])]
+            store(v, n, level[0])
 
 
 def lanes():
@@ -245,9 +265,15 @@
     return pl.ds(pl.multiple_of((2 * t + rg // 2) * PITCH + 8 * (rg % 2), 8), 8)
 
 
-def prepare_kernel(recv, vel_other, table, start, index, coefs, zero, nat, natv):
+def prepare_kernel(
+    recv, vel_other, table, start, index, coefs, row_table, zero, nat, natv
+):
     x, _, _, _, core = coordinates()
     zero[...] = jnp.zeros_like(zero)
+    entry = lax.broadcasted_iota(jnp.int32, (8, 128), 0) + jnp.where(lanes() < 64, 0, NV)
+    for j in range(8):
+        for n in range(BY_ROW):
+            row_table[n, j] = gather_lanes(table[n], entry + 8 * j)
     half = x // 2
     shift = jnp.where(lanes() < 64, 0, NV)
 
@@ -287,10 +313,10 @@
     def _(depth):
         @pl.loop(0, OWN, unroll=16)
         def _(i):
-            for v in range(4):
-                idx = natv[depth, v, block(i), :]
-                for n in range(COEFS):
-                    coefs[depth, i, v, n] = gather_lanes(table[n], idx)
+            def store(v, n, value):
+                coefs[depth, i, v, n] = value
+
+            look_up([natv[depth, v, block(i), :] for v in range(4)], table, row_table, store)
 
 
 def prepare(recv, vel_other, table):
@@ -301,10 +327,11 @@
             jax.ShapeDtypeStruct((2, OWN, 4, 8, 128), jnp.float32),
             jax.ShapeDtypeStruct((DEPTHS - AHEAD, OWN, 4, 8, 128), jnp.int32),
             jax.ShapeDtypeStruct((AHEAD, OWN, 4, COEFS, 8, 128), jnp.float32),
+            jax.ShapeDtypeStruct((BY_ROW, 8, 8, 128), jnp.float32),
             jax.ShapeDtypeStruct((8, 128), jnp.float32),
         ),
         in_specs=[vmem] * 3,
-        out_specs=(vmem,) * 4,
+        out_specs=(vmem,) * 5,
         scratch_shapes=[
             pltpu.VMEM((2, 4, 8 * PITCH, 128), jnp.float32),
             pltpu.VMEM((DEPTHS, 4, 8 * PITCH, 128), jnp.int32),
@@ -314,27 +341,27 @@
     )(recv, vel_other, table)
 
 
-def late_kernel(index, table, coefs):
+def late_kernel(index, table, row_table, coefs):
     for depth in range(DEPTHS - AHEAD):
 
         @pl.loop(0, OWN, unroll=16)
         def _(i):
-            for v in range(4):
-                idx = index[depth, i, v]
-                for n in range(COEFS):
-                    coefs[depth, i, v, n] = gather_lanes(table[n], idx)
-
-
-def late(index, table):
+            def store(v, n, value):
+                coefs[depth, i, v, n] = value
+
+            look_up([index[depth, i, v] for v in range(4)], table, row_table, store)
+
+
+def late(index, table, row_table):
     vmem = pl.BlockSpec(memory_space=pltpu.VMEM)
     return pl.pallas_call(
         late_kernel,
         out_shape=jax.ShapeDtypeStruct((DEPTHS - AHEAD, OWN, 4, COEFS, 8, 128), jnp.float32),
-        in_specs=[vmem] * 2,
+        in_specs=[vmem] * 3,
         out_specs=vmem,
         compiler_params=pltpu.CompilerParams(vmem_limit_bytes=8 * 1024 * 1024),
         cost_estimate=pl.CostEstimate(flops=5_000_000, bytes_accessed=1_000_000, transcendentals=0),
-    )(index, table)
+    )(index, table, row_table)
 
 
 def kernel(
@@ -584,11 +611,11 @@
     with jax.named_scope("velocity"):
         vel_other = lax.ppermute(recv[:, 2], AXES, core_pairs())
     with jax.named_scope("prepare"):
-        start, index, coefs, zero = prepare(recv, vel_other, table)
+        start, index, coefs, row_table, zero = prepare(recv, vel_other, table)
     with jax.named_scope("velocity"):
         edge_vel = lax.ppermute(edge_velocity(below, beside, corner, zero), AXES, core_pairs())
     with jax.named_scope("late"):
-        late_coefs = late(index, table)
+        late_coefs = late(index, table, row_table)
     with jax.named_scope("extrapolate"):
         out = extrapolate(start, late_coefs, coefs, below, beside, corner, edge_vel, table)
     with jax.named_scope("image"):

time: 67.8 us -> 66.6 us (0.982)
  Pallas kernels: 27.2 us -> 26 us
    pallas_call x1, Pallas kernels: 6.76 us -> 5.9 us  [prepare(): pl.pallas_call(prepare_kernel, out_shape=(jax.ShapeDtypeStruct((2, OWN, 4...]
  transfers between devices with their start and end apart: 7 -> 7, of which waited for: 2 -> 3; matrix products, arithmetic and copies ran while one was open for 0% -> 0% of each run, Pallas kernels for 13% -> 11%
where the time goes in v6:
time: 66.6 us; the launch traced here: 66.3 us
  Pallas kernels  26 us (39%)
  starting transfers between devices  14.1 us (21%)
  waiting for transfers between devices  14.1 us (21%)
  blocking collectives  11.9 us (18%)
    pallas_call x1, Pallas kernels, extrapolate(): pl.pallas_call(kernel, out_shape=jax.ShapeDtypeStruct((2, 16, 32, 128), j...  15.7 us
    all_to_all x1, waiting for transfers between devices, per_device(): recv = lax.all_to_all(send, AXES, 0, 0, axis_index_groups=groups)  12.8 us
    all_to_all x1, blocking collectives, per_device(): parts = lax.all_to_all(total, AXES, 0, 0, axis_index_groups=groups)  11.9 us
    all_to_all x1, starting transfers between devices, per_device(): recv = lax.all_to_all(send, AXES, 0, 0, axis_index_groups=groups)  7.45 us
    pallas_call x1, Pallas kernels, prepare(): pl.pallas_call(prepare_kernel, out_shape=(jax.ShapeDtypeStruct((2, OWN, 4...  5.9 us
    pallas_call x1, Pallas kernels, pack(): pl.pallas_call(pack_kernel, out_shape=jax.ShapeDtypeStruct((16, 3, 32, 12...  2.31 us
    ppermute x1, starting transfers between devices, per_device(): lax.ppermute(beside, AXES, pairs(lambda x, y, *rest: (x, 3 - y, *rest)))  2.18 us
    ppermute x1, starting transfers between devices, per_device(): lax.ppermute(below, AXES, pairs(lambda x, y, *rest: (3 - x, y, *rest)))  2.18 us
  transfers between devices with their start and end apart: 7, of which 3 were waited for; matrix products, arithmetic and copies ran while one was open for 0% of the time, Pallas kernels for 11%

profile of v6, /device:TPU:0, one launch (start us, length us, event | category | flops | bytes accessed | tf_op | source)
XLA Modules:
  0.0 66.3 jit_solution(14443232341808457236)
XLA Ops:
  0.0 0.0 copy-start
  0.0 2.3 %pack.1 = f32[16,3,32,128]{3,2,1,0:T(8,128)} custom-call(f32[32,2,2,32,128]{4,3,2,1,0:T(8,128)} %bitcast.11, s32[1,32,128]{2,1,0:T(8,128)} %vel.1), custom_call_target="tpu_custom_call" | custom-call | tf_op jit(solution)/shard_map/pack/pallas_call | solution.py:143
  2.3 7.5 %all-to-all-start = ((f32[16,3,32,128]{3,2,1,0:T(8,128)}), f32[16,3,32,128]{3,2,1,0:T(8,128)S(1)}, u32[]{:S(2)}, u32[]{:S(2)}) async-start(f32[16,3,32,128]{3,2,1,0:T(8,128)} %pack.1), calls=%async_computation | async-start | bytes 1572864 | tf_op jit(solution)/shard_map/spread/all_to_all | solution.py:605
  9.8 12.8 %all-to-all-done.recv = f32[16,3,32,128]{3,2,1,0:T(8,128)S(1)} async-done(((f32[16,3,32,128]{3,2,1,0:T(8,128)}), f32[16,3,32,128]{3,2,1,0:T(8,128)S(1)}, u32[]{:S(2)}, u32[]{:S(2)}) %all-to-all-start) | async-done | bytes 786464 | tf_op jit(solution)/shard_map/spread/all_to_all | solution.py:605
  22.6 0.1 collective-permute-start
  22.7 0.0 copy-done
  22.8 0.2 halo.1
  23.0 2.2 %collective-permute-start.1 = (f32[10,32,128]{2,1,0:T(8,128)S(1)}, f32[10,32,128]{2,1,0:T(8,128)S(1)}, u32[]{:S(2)}, u32[]{:S(2)}) collective-permute-start(f32[10,32,128]{2,1,0:T(8,128)S(1)} %get-tuple-element.19), channel_id=1, source_target_pairs={{0,24},{32,56},{64,88},{96,120},{4,28},{36,60},{68,92},{100,124},{... | collective-permute-start | bytes 491528 | tf_op jit(solution)/shard_map/halo/ppermute | solution.py:608
  25.2 2.2 %collective-permute-start.2 = (f32[3,64,128]{2,1,0:T(8,128)S(1)}, f32[3,64,128]{2,1,0:T(8,128)S(1)}, u32[]{:S(2)}, u32[]{:S(2)}) collective-permute-start(f32[3,64,128]{2,1,0:T(8,128)S(1)} %get-tuple-element.20), channel_id=1, source_target_pairs={{0,3},{32,35},{64,67},{96,99},{4,7},{36,39},{68,71},{100,103},{1,2... | collective-permute-start | bytes 294920 | tf_op jit(solution)/shard_map/halo/ppermute | solution.py:609
  27.4 1.6 %collective-permute-start.3 = (f32[3,32,128]{2,1,0:T(8,128)S(1)}, f32[3,32,128]{2,1,0:T(8,128)S(1)}, u32[]{:S(2)}, u32[]{:S(2)}) collective-permute-start(f32[3,32,128]{2,1,0:T(8,128)S(1)} %get-tuple-element.21), channel_id=1, source_target_pairs={{0,27},{32,59},{64,91},{96,123},{4,31},{36,63},{68,95},{100,127},{... | collective-permute-start | bytes 147464 | tf_op jit(solution)/shard_map/halo/ppermute | solution.py:610
  29.0 0.0 collective-permute-done.vel_other
  29.0 5.9 %prepare.1 = (f32[2,16,4,8,128]{4,3,2,1,0:T(8,128)S(1)}, s32[1,16,4,8,128]{4,3,2,1,0:T(8,128)S(1)}, f32[3,16,4,18,8,128]{5,4,3,2,1,0:T(8,128)S(1)}, f32[6,8,8,128]{3,2,1,0:T(8,128)S(1)}, f32[8,128]{1,0:T(8,128)S(1)}) custom-call(f32[16,3,32,128]{3,2,1,0:T(8,128)S(1)} %all-to-all-done.recv, f32[16,32,128]{2,1,0:T(8,128)S(1)} %collective-permute-done.vel_other, ...), custom_call_target="tpu_custom_call" | custom-call | flops 20000000 | bytes 4000000 | tf_op jit(solution)/shard_map/prepare/pallas_call | solution.py:324
  34.9 0.0 collective-permute-done.3.corner
  34.9 0.0 collective-permute-done.2.beside
  34.9 0.0 collective-permute-done.1.below
  34.9 0.1 collective-permute-start.4
  35.0 1.1 %late.1.late_coefs = f32[1,16,4,18,8,128]{5,4,3,2,1,0:T(8,128)S(1)} custom-call(s32[1,16,4,8,128]{4,3,2,1,0:T(8,128)S(1)} %get-tuple-element.16.index, f32[18,8,128]{2,1,0:T(8,128)S(1)} %get-tuple-element.14.table, f32[6,8,8,128]{3,2,1,0:T(8,128)S(1)} %get-tuple-element.17.row_table), custom_call_target="tpu_custom_call" | custom-call | flops 5000000 | bytes 1000000 | tf_op jit(solution)/shard_map/late/pallas_call | solution.py:357
  36.2 0.1 collective-permute-done.4.vel_other
  36.3 15.7 %extrapolate.1 = f32[2,16,32,128]{3,2,1,0:T(8,128)S(1)} custom-call(f32[2,16,4,8,128]{4,3,2,1,0:T(8,128)S(1)} %get-tuple-element.15.start, f32[1,16,4,18,8,128]{5,4,3,2,1,0:T(8,128)S(1)} %late.1.late_coefs, f32[3,16,4,18,8,128]{5,4,3,2,1,0:T(8,128)S(1)} %get-tuple-element.18.coefs, f32[10,32,128]{2,1,0:T(8,128)S(1)} %collective-permute-done.1.below, ...), custom_call_target="tpu_custom_call" | custom-call | flops 70000000 | bytes 4000000 | tf_op jit(solution)/shard_map/extrapolate/pallas_call | solution.py:574
  52.1 0.5 collective-permute-start.5
  52.5 1.2 %collective-permute-done.5 = f32[16,32,128]{2,1,0:T(8,128)S(1)} collective-permute-done((f32[16,32,128]{2,1,0:T(8,128)S(1)}, f32[16,32,128]{2,1,0:T(8,128)S(1)}, u32[]{:S(2)}, u32[]{:S(2)}) %collective-permute-start.5) | collective-permute-done | bytes 262176 | tf_op jit(solution)/shard_map/image/ppermute | solution.py:622
  53.8 11.9 %all_to_all.10.parts = f32[16,32,128]{2,1,0:T(8,128)S(1)} all-to-all(f32[16,32,128]{2,1,0:T(8,128)S(1)} %fusion), channel_id=1, replica_groups={{0,1,64,65,4,5,68,69,8,9,72,73,12,13,76,77},{32,33,96,97,36,37,100,101,..., dimensions={0} | all-to-all | bytes 524288 | tf_op jit(solution)/shard_map/image/all_to_all | solution.py:623
  65.6 0.7 %image.1 = f32[1,32,128]{2,1,0:T(8,128)} custom-call(f32[16,32,128]{2,1,0:T(8,128)S(1)} %all_to_all.10.parts), custom_call_target="tpu_custom_call" | custom-call | tf_op jit(solution)/shard_map/image/pallas_call | solution.py:171
  (5 shorter events, 0.1 us)
Async XLA Ops:
  0.0 22.7 %copy-start = (f32[64,9,2,64]{3,2,1,0:T(2,128)S(1)}, f32[64,9,2,64]{3,2,1,0:T(2,128)}, u32[]{:S(2)}) copy-start(f32[64,9,2,64]{3,2,1,0:T(2,128)} %param.4) | copy-start | bytes 884740
  2.3 20.3 %all-to-all-start = ((f32[16,3,32,128]{3,2,1,0:T(8,128)}), f32[16,3,32,128]{3,2,1,0:T(8,128)S(1)}, u32[]{:S(2)}, u32[]{:S(2)}) async-start(f32[16,3,32,128]{3,2,1,0:T(8,128)} %pack.1), calls=%async_computation | async-start | bytes 1572864 | tf_op jit(solution)/shard_map/spread/all_to_all | solution.py:605
  22.6 6.3 %collective-permute-start = (f32[16,32,128]{2,1,0:T(8,128)S(1)}, f32[16,32,128]{2,1,0:T(8,128)S(1)}, u32[]{:S(2)}, u32[]{:S(2)}) collective-permute-start(f32[16,32,128]{2,1,0:T(8,128)S(1)} %slice_bitcast_fusion.2), channel_id=1, source_target_pairs={{0,32},{32,0},{64,96},{96,64},{4,36},{36,4},{68,100},{100,68},{1,3... | collective-permute-start | bytes 786440 | tf_op jit(solution)/shard_map/velocity/ppermute | solution.py:612
  23.0 11.9 %collective-permute-start.1 = (f32[10,32,128]{2,1,0:T(8,128)S(1)}, f32[10,32,128]{2,1,0:T(8,128)S(1)}, u32[]{:S(2)}, u32[]{:S(2)}) collective-permute-start(f32[10,32,128]{2,1,0:T(8,128)S(1)} %get-tuple-element.19), channel_id=1, source_target_pairs={{0,24},{32,56},{64,88},{96,120},{4,28},{36,60},{68,92},{100,124},{... | collective-permute-start | bytes 491528 | tf_op jit(solution)/shard_map/halo/ppermute | solution.py:608
  25.2 9.7 %collective-permute-start.2 = (f32[3,64,128]{2,1,0:T(8,128)S(1)}, f32[3,64,128]{2,1,0:T(8,128)S(1)}, u32[]{:S(2)}, u32[]{:S(2)}) collective-permute-start(f32[3,64,128]{2,1,0:T(8,128)S(1)} %get-tuple-element.20), channel_id=1, source_target_pairs={{0,3},{32,35},{64,67},{96,99},{4,7},{36,39},{68,71},{100,103},{1,2... | collective-permute-start | bytes 294920 | tf_op jit(solution)/shard_map/halo/ppermute | solution.py:609
  27.4 7.5 %collective-permute-start.3 = (f32[3,32,128]{2,1,0:T(8,128)S(1)}, f32[3,32,128]{2,1,0:T(8,128)S(1)}, u32[]{:S(2)}, u32[]{:S(2)}) collective-permute-start(f32[3,32,128]{2,1,0:T(8,128)S(1)} %get-tuple-element.21), channel_id=1, source_target_pairs={{0,27},{32,59},{64,91},{96,123},{4,31},{36,63},{68,95},{100,127},{... | collective-permute-start | bytes 147464 | tf_op jit(solution)/shard_map/halo/ppermute | solution.py:610
  34.9 1.4 %collective-permute-start.4 = (f32[5,32,128]{2,1,0:T(8,128)S(1)}, f32[5,32,128]{2,1,0:T(8,128)S(1)}, u32[]{:S(2)}, u32[]{:S(2)}) collective-permute-start(f32[5,32,128]{2,1,0:T(8,128)S(1)} %velocity.1), channel_id=1, source_target_pairs={{0,32},{32,0},{64,96},{96,64},{4,36},{36,4},{68,100},{100,68},{1,3... | collective-permute-start | bytes 245768 | tf_op jit(solution)/shard_map/velocity/ppermute | solution.py:616
  52.1 1.6 %collective-permute-start.5 = (f32[16,32,128]{2,1,0:T(8,128)S(1)}, f32[16,32,128]{2,1,0:T(8,128)S(1)}, u32[]{:S(2)}, u32[]{:S(2)}) collective-permute-start(f32[16,32,128]{2,1,0:T(8,128)S(1)} %slice_bitcast_fusion), channel_id=1, source_target_pairs={{0,32},{32,0},{64,96},{96,64},{4,36},{36,4},{68,100},{100,68},{1,3... | collective-permute-start | bytes 786440 | tf_op jit(solution)/shard_map/image/ppermute | solution.py:622

commit v7 on v6

--- a/solution.py
+++ b/solution.py
@@ -15,6 +15,7 @@
 DEPTHS = 4
 NV = 64
 COEFS = 2 * (TOP + 1)
+HALO_BY_ROW = 4
 BY_ROW = 6
 
 
@@ -365,7 +366,7 @@
 
 
 def kernel(
-    start, late_coefs, coefs, below, beside, corner, vel_other, table, out,
+    start, late_coefs, coefs, below, beside, corner, vel_other, table, row_table, out,
     nat, natv, side, sidev, term, pair_sum, img
 ):
     x, _, _, _, core = coordinates()
@@ -506,6 +507,20 @@
         term[0, 1, i, v] = imag
         return real
 
+    def halo_coef(idx):
+        low = idx & 7
+        bits = [(idx & (8 << b)) == 0 for b in range(3)]
+
+        def coef(n):
+            if n >= HALO_BY_ROW:
+                return gather_lanes(table[n], idx)
+            level = [gather_rows(row_table[n, j], low) for j in range(8)]
+            for bit in bits:
+                level = [jnp.where(bit, a, b) for a, b in zip(level[::2], level[1::2])]
+            return level[0]
+
+        return coef
+
     @pl.loop(0, DEPTHS)
     def _(depth):
         for part in range(2):
@@ -549,10 +564,10 @@
             for j in range(BLK - OWN):
                 for v in range(WAYS):
                     idx = natv[depth, v, pl.ds(j, 8, stride=4), :]
-                    combine(OWN + j, v, lambda n: gather_lanes(table[n], idx))
+                    combine(OWN + j, v, halo_coef(idx))
             for i in range(OWN):
                 idx = sidev[depth, block(i), :]
-                combine(i, 4, lambda n: gather_lanes(table[n], idx))
+                combine(i, 4, halo_coef(idx))
 
         slot = jnp.where(depth % 2 == core, 0, 1)
         zl = depth // 2
@@ -574,7 +589,7 @@
     return pl.pallas_call(
         kernel,
         out_shape=jax.ShapeDtypeStruct((2, 16, 32, 128), jnp.float32),
-        in_specs=[vmem] * 8,
+        in_specs=[vmem] * 9,
         out_specs=vmem,
         scratch_shapes=[
             pltpu.VMEM((2, WAYS, 32, 128), jnp.float32),
@@ -617,7 +632,9 @@
     with jax.named_scope("late"):
         late_coefs = late(index, table, row_table)
     with jax.named_scope("extrapolate"):
-        out = extrapolate(start, late_coefs, coefs, below, beside, corner, edge_vel, table)
+        out = extrapolate(
+            start, late_coefs, coefs, below, beside, corner, edge_vel, table, row_table
+        )
     with jax.named_scope("image"):
         total = out[0] + lax.ppermute(out[1], AXES, core_pairs())
         parts = lax.all_to_all(total, AXES, 0, 0, axis_index_groups=groups)

time: 66.6 us -> 66.4 us (level)
  no operation moved by 1% of the time
where the time goes in v7:
time: 66.4 us; the launch traced here: 66.1 us
  Pallas kernels  25.9 us (39%)
  starting transfers between devices  14.1 us (21%)
  waiting for transfers between devices  14.1 us (21%)
  blocking collectives  11.9 us (18%)
    pallas_call x1, Pallas kernels, extrapolate(): pl.pallas_call(kernel, out_shape=jax.ShapeDtypeStruct((2, 16, 32, 128), j...  15.6 us
    all_to_all x1, waiting for transfers between devices, per_device(): recv = lax.all_to_all(send, AXES, 0, 0, axis_index_groups=groups)  12.8 us
    all_to_all x1, blocking collectives, per_device(): parts = lax.all_to_all(total, AXES, 0, 0, axis_index_groups=groups)  11.9 us
    all_to_all x1, starting transfers between devices, per_device(): recv = lax.all_to_all(send, AXES, 0, 0, axis_index_groups=groups)  7.45 us
    pallas_call x1, Pallas kernels, prepare(): pl.pallas_call(prepare_kernel, out_shape=(jax.ShapeDtypeStruct((2, OWN, 4...  5.9 us
    pallas_call x1, Pallas kernels, pack(): pl.pallas_call(pack_kernel, out_shape=jax.ShapeDtypeStruct((16, 3, 32, 12...  2.31 us
    ppermute x1, starting transfers between devices, per_device(): lax.ppermute(beside, AXES, pairs(lambda x, y, *rest: (x, 3 - y, *rest)))  2.18 us
    ppermute x1, starting transfers between devices, per_device(): lax.ppermute(below, AXES, pairs(lambda x, y, *rest: (3 - x, y, *rest)))  2.18 us
  transfers between devices with their start and end apart: 7, of which 3 were waited for; matrix products, arithmetic and copies ran while one was open for 0% of the time, Pallas kernels for 11%

profile of v7, /device:TPU:0, one launch (start us, length us, event | category | flops | bytes accessed | tf_op | source)
XLA Modules:
  0.0 66.1 jit_solution(4288361471797338524)
XLA Ops:
  0.0 0.0 copy-start
  0.0 2.3 %pack.1 = f32[16,3,32,128]{3,2,1,0:T(8,128)} custom-call(f32[32,2,2,32,128]{4,3,2,1,0:T(8,128)} %bitcast.11, s32[1,32,128]{2,1,0:T(8,128)} %vel.1), custom_call_target="tpu_custom_call" | custom-call | tf_op jit(solution)/shard_map/pack/pallas_call | solution.py:144
  2.3 7.5 %all-to-all-start = ((f32[16,3,32,128]{3,2,1,0:T(8,128)}), f32[16,3,32,128]{3,2,1,0:T(8,128)S(1)}, u32[]{:S(2)}, u32[]{:S(2)}) async-start(f32[16,3,32,128]{3,2,1,0:T(8,128)} %pack.1), calls=%async_computation | async-start | bytes 1572864 | tf_op jit(solution)/shard_map/spread/all_to_all | solution.py:620
  9.8 12.8 %all-to-all-done.recv = f32[16,3,32,128]{3,2,1,0:T(8,128)S(1)} async-done(((f32[16,3,32,128]{3,2,1,0:T(8,128)}), f32[16,3,32,128]{3,2,1,0:T(8,128)S(1)}, u32[]{:S(2)}, u32[]{:S(2)}) %all-to-all-start) | async-done | bytes 786464 | tf_op jit(solution)/shard_map/spread/all_to_all | solution.py:620
  22.6 0.1 collective-permute-start
  22.7 0.0 copy-done
  22.8 0.2 halo.1
  23.0 2.2 %collective-permute-start.1 = (f32[10,32,128]{2,1,0:T(8,128)S(1)}, f32[10,32,128]{2,1,0:T(8,128)S(1)}, u32[]{:S(2)}, u32[]{:S(2)}) collective-permute-start(f32[10,32,128]{2,1,0:T(8,128)S(1)} %get-tuple-element.19), channel_id=1, source_target_pairs={{0,24},{32,56},{64,88},{96,120},{4,28},{36,60},{68,92},{100,124},{... | collective-permute-start | bytes 491528 | tf_op jit(solution)/shard_map/halo/ppermute | solution.py:623
  25.2 2.2 %collective-permute-start.2 = (f32[3,64,128]{2,1,0:T(8,128)S(1)}, f32[3,64,128]{2,1,0:T(8,128)S(1)}, u32[]{:S(2)}, u32[]{:S(2)}) collective-permute-start(f32[3,64,128]{2,1,0:T(8,128)S(1)} %get-tuple-element.20), channel_id=1, source_target_pairs={{0,3},{32,35},{64,67},{96,99},{4,7},{36,39},{68,71},{100,103},{1,2... | collective-permute-start | bytes 294920 | tf_op jit(solution)/shard_map/halo/ppermute | solution.py:624
  27.4 1.6 %collective-permute-start.3 = (f32[3,32,128]{2,1,0:T(8,128)S(1)}, f32[3,32,128]{2,1,0:T(8,128)S(1)}, u32[]{:S(2)}, u32[]{:S(2)}) collective-permute-start(f32[3,32,128]{2,1,0:T(8,128)S(1)} %get-tuple-element.21), channel_id=1, source_target_pairs={{0,27},{32,59},{64,91},{96,123},{4,31},{36,63},{68,95},{100,127},{... | collective-permute-start | bytes 147464 | tf_op jit(solution)/shard_map/halo/ppermute | solution.py:625
  29.0 0.0 collective-permute-done.vel_other
  29.0 5.9 %prepare.1 = (f32[2,16,4,8,128]{4,3,2,1,0:T(8,128)S(1)}, s32[1,16,4,8,128]{4,3,2,1,0:T(8,128)S(1)}, f32[3,16,4,18,8,128]{5,4,3,2,1,0:T(8,128)S(1)}, f32[6,8,8,128]{3,2,1,0:T(8,128)S(1)}, f32[8,128]{1,0:T(8,128)S(1)}) custom-call(f32[16,3,32,128]{3,2,1,0:T(8,128)S(1)} %all-to-all-done.recv, f32[16,32,128]{2,1,0:T(8,128)S(1)} %collective-permute-done.vel_other, ...), custom_call_target="tpu_custom_call" | custom-call | flops 20000000 | bytes 4000000 | tf_op jit(solution)/shard_map/prepare/pallas_call | solution.py:325
  34.9 0.0 collective-permute-done.3.corner
  34.9 0.0 collective-permute-done.2.beside
  34.9 0.0 collective-permute-done.1.below
  34.9 0.1 collective-permute-start.4
  35.0 1.1 %late.1.late_coefs = f32[1,16,4,18,8,128]{5,4,3,2,1,0:T(8,128)S(1)} custom-call(s32[1,16,4,8,128]{4,3,2,1,0:T(8,128)S(1)} %get-tuple-element.16.index, f32[18,8,128]{2,1,0:T(8,128)S(1)} %get-tuple-element.14.table, f32[6,8,8,128]{3,2,1,0:T(8,128)S(1)} %get-tuple-element.17.row_table), custom_call_target="tpu_custom_call" | custom-call | flops 5000000 | bytes 1000000 | tf_op jit(solution)/shard_map/late/pallas_call | solution.py:358
  36.2 0.1 collective-permute-done.4.vel_other
  36.3 15.6 %extrapolate.1 = f32[2,16,32,128]{3,2,1,0:T(8,128)S(1)} custom-call(f32[2,16,4,8,128]{4,3,2,1,0:T(8,128)S(1)} %get-tuple-element.15.start, f32[1,16,4,18,8,128]{5,4,3,2,1,0:T(8,128)S(1)} %late.1.late_coefs, f32[3,16,4,18,8,128]{5,4,3,2,1,0:T(8,128)S(1)} %get-tuple-element.18.coefs, f32[10,32,128]{2,1,0:T(8,128)S(1)} %collective-permute-done.1.below, ...), custom_call_target="tpu_custom_call" | custom-call | flops 70000000 | bytes 4000000 | tf_op jit(solution)/shard_map/extrapolate/pallas_call | solution.py:589
  51.9 0.5 collective-permute-start.5
  52.4 1.2 %collective-permute-done.5 = f32[16,32,128]{2,1,0:T(8,128)S(1)} collective-permute-done((f32[16,32,128]{2,1,0:T(8,128)S(1)}, f32[16,32,128]{2,1,0:T(8,128)S(1)}, u32[]{:S(2)}, u32[]{:S(2)}) %collective-permute-start.5) | collective-permute-done | bytes 262176 | tf_op jit(solution)/shard_map/image/ppermute | solution.py:639
  53.6 11.9 %all_to_all.10.parts = f32[16,32,128]{2,1,0:T(8,128)S(1)} all-to-all(f32[16,32,128]{2,1,0:T(8,128)S(1)} %fusion), channel_id=1, replica_groups={{0,1,64,65,4,5,68,69,8,9,72,73,12,13,76,77},{32,33,96,97,36,37,100,101,..., dimensions={0} | all-to-all | bytes 524288 | tf_op jit(solution)/shard_map/image/all_to_all | solution.py:640
  65.4 0.7 %image.1 = f32[1,32,128]{2,1,0:T(8,128)} custom-call(f32[16,32,128]{2,1,0:T(8,128)S(1)} %all_to_all.10.parts), custom_call_target="tpu_custom_call" | custom-call | tf_op jit(solution)/shard_map/image/pallas_call | solution.py:172
  (5 shorter events, 0.1 us)
Async XLA Ops:
  0.0 22.7 %copy-start = (f32[64,9,2,64]{3,2,1,0:T(2,128)S(1)}, f32[64,9,2,64]{3,2,1,0:T(2,128)}, u32[]{:S(2)}) copy-start(f32[64,9,2,64]{3,2,1,0:T(2,128)} %param.4) | copy-start | bytes 884740
  2.3 20.3 %all-to-all-start = ((f32[16,3,32,128]{3,2,1,0:T(8,128)}), f32[16,3,32,128]{3,2,1,0:T(8,128)S(1)}, u32[]{:S(2)}, u32[]{:S(2)}) async-start(f32[16,3,32,128]{3,2,1,0:T(8,128)} %pack.1), calls=%async_computation | async-start | bytes 1572864 | tf_op jit(solution)/shard_map/spread/all_to_all | solution.py:620
  22.6 6.3 %collective-permute-start = (f32[16,32,128]{2,1,0:T(8,128)S(1)}, f32[16,32,128]{2,1,0:T(8,128)S(1)}, u32[]{:S(2)}, u32[]{:S(2)}) collective-permute-start(f32[16,32,128]{2,1,0:T(8,128)S(1)} %slice_bitcast_fusion.2), channel_id=1, source_target_pairs={{0,32},{32,0},{64,96},{96,64},{4,36},{36,4},{68,100},{100,68},{1,3... | collective-permute-start | bytes 786440 | tf_op jit(solution)/shard_map/velocity/ppermute | solution.py:627
  23.0 11.9 %collective-permute-start.1 = (f32[10,32,128]{2,1,0:T(8,128)S(1)}, f32[10,32,128]{2,1,0:T(8,128)S(1)}, u32[]{:S(2)}, u32[]{:S(2)}) collective-permute-start(f32[10,32,128]{2,1,0:T(8,128)S(1)} %get-tuple-element.19), channel_id=1, source_target_pairs={{0,24},{32,56},{64,88},{96,120},{4,28},{36,60},{68,92},{100,124},{... | collective-permute-start | bytes 491528 | tf_op jit(solution)/shard_map/halo/ppermute | solution.py:623
  25.2 9.7 %collective-permute-start.2 = (f32[3,64,128]{2,1,0:T(8,128)S(1)}, f32[3,64,128]{2,1,0:T(8,128)S(1)}, u32[]{:S(2)}, u32[]{:S(2)}) collective-permute-start(f32[3,64,128]{2,1,0:T(8,128)S(1)} %get-tuple-element.20), channel_id=1, source_target_pairs={{0,3},{32,35},{64,67},{96,99},{4,7},{36,39},{68,71},{100,103},{1,2... | collective-permute-start | bytes 294920 | tf_op jit(solution)/shard_map/halo/ppermute | solution.py:624
  27.4 7.5 %collective-permute-start.3 = (f32[3,32,128]{2,1,0:T(8,128)S(1)}, f32[3,32,128]{2,1,0:T(8,128)S(1)}, u32[]{:S(2)}, u32[]{:S(2)}) collective-permute-start(f32[3,32,128]{2,1,0:T(8,128)S(1)} %get-tuple-element.21), channel_id=1, source_target_pairs={{0,27},{32,59},{64,91},{96,123},{4,31},{36,63},{68,95},{100,127},{... | collective-permute-start | bytes 147464 | tf_op jit(solution)/shard_map/halo/ppermute | solution.py:625
  34.9 1.4 %collective-permute-start.4 = (f32[5,32,128]{2,1,0:T(8,128)S(1)}, f32[5,32,128]{2,1,0:T(8,128)S(1)}, u32[]{:S(2)}, u32[]{:S(2)}) collective-permute-start(f32[5,32,128]{2,1,0:T(8,128)S(1)} %velocity.1), channel_id=1, source_target_pairs={{0,32},{32,0},{64,96},{96,64},{4,36},{36,4},{68,100},{100,68},{1,3... | collective-permute-start | bytes 245768 | tf_op jit(solution)/shard_map/velocity/ppermute | solution.py:631
  51.9 1.6 %collective-permute-start.5 = (f32[16,32,128]{2,1,0:T(8,128)S(1)}, f32[16,32,128]{2,1,0:T(8,128)S(1)}, u32[]{:S(2)}, u32[]{:S(2)}) collective-permute-start(f32[16,32,128]{2,1,0:T(8,128)S(1)} %slice_bitcast_fusion), channel_id=1, source_target_pairs={{0,32},{32,0},{64,96},{96,64},{4,36},{36,4},{68,100},{100,68},{1,3... | collective-permute-start | bytes 786440 | tf_op jit(solution)/shard_map/image/ppermute | solution.py:639

commit v8 on v7

--- a/solution.py
+++ b/solution.py
@@ -15,7 +15,7 @@
 DEPTHS = 4
 NV = 64
 COEFS = 2 * (TOP + 1)
-HALO_BY_ROW = 4
+HALO_BY_ROW = 6
 BY_ROW = 6
 
 

time: 66.4 us -> 66.6 us (level)
  no operation moved by 1% of the time
where the time goes in v8:
time: 66.6 us; the launch traced here: 66.4 us
  Pallas kernels  26.1 us (39%)
  starting transfers between devices  14.1 us (21%)
  waiting for transfers between devices  14.1 us (21%)
  blocking collectives  11.9 us (18%)
    pallas_call x1, Pallas kernels, extrapolate(): pl.pallas_call(kernel, out_shape=jax.ShapeDtypeStruct((2, 16, 32, 128), j...  15.8 us
    all_to_all x1, waiting for transfers between devices, per_device(): recv = lax.all_to_all(send, AXES, 0, 0, axis_index_groups=groups)  12.8 us
    all_to_all x1, blocking collectives, per_device(): parts = lax.all_to_all(total, AXES, 0, 0, axis_index_groups=groups)  11.9 us
    all_to_all x1, starting transfers between devices, per_device(): recv = lax.all_to_all(send, AXES, 0, 0, axis_index_groups=groups)  7.45 us
    pallas_call x1, Pallas kernels, prepare(): pl.pallas_call(prepare_kernel, out_shape=(jax.ShapeDtypeStruct((2, OWN, 4...  5.9 us
    pallas_call x1, Pallas kernels, pack(): pl.pallas_call(pack_kernel, out_shape=jax.ShapeDtypeStruct((16, 3, 32, 12...  2.31 us
    ppermute x1, starting transfers between devices, per_device(): lax.ppermute(beside, AXES, pairs(lambda x, y, *rest: (x, 3 - y, *rest)))  2.18 us
    ppermute x1, starting transfers between devices, per_device(): lax.ppermute(below, AXES, pairs(lambda x, y, *rest: (3 - x, y, *rest)))  2.18 us
  transfers between devices with their start and end apart: 7, of which 3 were waited for; matrix products, arithmetic and copies ran while one was open for 0% of the time, Pallas kernels for 11%

profile of v8, /device:TPU:0, one launch (start us, length us, event | category | flops | bytes accessed | tf_op | source)
XLA Modules:
  0.0 66.4 jit_solution(3173679849656928236)
XLA Ops:
  0.0 0.0 copy-start
  0.0 2.3 %pack.1 = f32[16,3,32,128]{3,2,1,0:T(8,128)} custom-call(f32[32,2,2,32,128]{4,3,2,1,0:T(8,128)} %bitcast.11, s32[1,32,128]{2,1,0:T(8,128)} %vel.1), custom_call_target="tpu_custom_call" | custom-call | tf_op jit(solution)/shard_map/pack/pallas_call | solution.py:144
  2.3 7.5 %all-to-all-start = ((f32[16,3,32,128]{3,2,1,0:T(8,128)}), f32[16,3,32,128]{3,2,1,0:T(8,128)S(1)}, u32[]{:S(2)}, u32[]{:S(2)}) async-start(f32[16,3,32,128]{3,2,1,0:T(8,128)} %pack.1), calls=%async_computation | async-start | bytes 1572864 | tf_op jit(solution)/shard_map/spread/all_to_all | solution.py:620
  9.8 12.8 %all-to-all-done.recv = f32[16,3,32,128]{3,2,1,0:T(8,128)S(1)} async-done(((f32[16,3,32,128]{3,2,1,0:T(8,128)}), f32[16,3,32,128]{3,2,1,0:T(8,128)S(1)}, u32[]{:S(2)}, u32[]{:S(2)}) %all-to-all-start) | async-done | bytes 786464 | tf_op jit(solution)/shard_map/spread/all_to_all | solution.py:620
  22.6 0.1 collective-permute-start
  22.7 0.0 copy-done
  22.8 0.2 halo.1
  23.0 2.2 %collective-permute-start.1 = (f32[10,32,128]{2,1,0:T(8,128)S(1)}, f32[10,32,128]{2,1,0:T(8,128)S(1)}, u32[]{:S(2)}, u32[]{:S(2)}) collective-permute-start(f32[10,32,128]{2,1,0:T(8,128)S(1)} %get-tuple-element.19), channel_id=1, source_target_pairs={{0,24},{32,56},{64,88},{96,120},{4,28},{36,60},{68,92},{100,124},{... | collective-permute-start | bytes 491528 | tf_op jit(solution)/shard_map/halo/ppermute | solution.py:623
  25.2 2.2 %collective-permute-start.2 = (f32[3,64,128]{2,1,0:T(8,128)S(1)}, f32[3,64,128]{2,1,0:T(8,128)S(1)}, u32[]{:S(2)}, u32[]{:S(2)}) collective-permute-start(f32[3,64,128]{2,1,0:T(8,128)S(1)} %get-tuple-element.20), channel_id=1, source_target_pairs={{0,3},{32,35},{64,67},{96,99},{4,7},{36,39},{68,71},{100,103},{1,2... | collective-permute-start | bytes 294920 | tf_op jit(solution)/shard_map/halo/ppermute | solution.py:624
  27.4 1.6 %collective-permute-start.3 = (f32[3,32,128]{2,1,0:T(8,128)S(1)}, f32[3,32,128]{2,1,0:T(8,128)S(1)}, u32[]{:S(2)}, u32[]{:S(2)}) collective-permute-start(f32[3,32,128]{2,1,0:T(8,128)S(1)} %get-tuple-element.21), channel_id=1, source_target_pairs={{0,27},{32,59},{64,91},{96,123},{4,31},{36,63},{68,95},{100,127},{... | collective-permute-start | bytes 147464 | tf_op jit(solution)/shard_map/halo/ppermute | solution.py:625
  29.0 0.0 collective-permute-done.vel_other
  29.0 5.9 %prepare.1 = (f32[2,16,4,8,128]{4,3,2,1,0:T(8,128)S(1)}, s32[1,16,4,8,128]{4,3,2,1,0:T(8,128)S(1)}, f32[3,16,4,18,8,128]{5,4,3,2,1,0:T(8,128)S(1)}, f32[6,8,8,128]{3,2,1,0:T(8,128)S(1)}, f32[8,128]{1,0:T(8,128)S(1)}) custom-call(f32[16,3,32,128]{3,2,1,0:T(8,128)S(1)} %all-to-all-done.recv, f32[16,32,128]{2,1,0:T(8,128)S(1)} %collective-permute-done.vel_other, ...), custom_call_target="tpu_custom_call" | custom-call | flops 20000000 | bytes 4000000 | tf_op jit(solution)/shard_map/prepare/pallas_call | solution.py:325
  34.9 0.0 collective-permute-done.3.corner
  34.9 0.0 collective-permute-done.2.beside
  34.9 0.0 collective-permute-done.1.below
  34.9 0.1 collective-permute-start.4
  35.0 1.1 %late.1.late_coefs = f32[1,16,4,18,8,128]{5,4,3,2,1,0:T(8,128)S(1)} custom-call(s32[1,16,4,8,128]{4,3,2,1,0:T(8,128)S(1)} %get-tuple-element.16.index, f32[18,8,128]{2,1,0:T(8,128)S(1)} %get-tuple-element.14.table, f32[6,8,8,128]{3,2,1,0:T(8,128)S(1)} %get-tuple-element.17.row_table), custom_call_target="tpu_custom_call" | custom-call | flops 5000000 | bytes 1000000 | tf_op jit(solution)/shard_map/late/pallas_call | solution.py:358
  36.2 0.1 collective-permute-done.4.vel_other
  36.3 15.8 %extrapolate.1 = f32[2,16,32,128]{3,2,1,0:T(8,128)S(1)} custom-call(f32[2,16,4,8,128]{4,3,2,1,0:T(8,128)S(1)} %get-tuple-element.15.start, f32[1,16,4,18,8,128]{5,4,3,2,1,0:T(8,128)S(1)} %late.1.late_coefs, f32[3,16,4,18,8,128]{5,4,3,2,1,0:T(8,128)S(1)} %get-tuple-element.18.coefs, f32[10,32,128]{2,1,0:T(8,128)S(1)} %collective-permute-done.1.below, ...), custom_call_target="tpu_custom_call" | custom-call | flops 70000000 | bytes 4000000 | tf_op jit(solution)/shard_map/extrapolate/pallas_call | solution.py:589
  52.2 0.5 collective-permute-start.5
  52.6 1.2 %collective-permute-done.5 = f32[16,32,128]{2,1,0:T(8,128)S(1)} collective-permute-done((f32[16,32,128]{2,1,0:T(8,128)S(1)}, f32[16,32,128]{2,1,0:T(8,128)S(1)}, u32[]{:S(2)}, u32[]{:S(2)}) %collective-permute-start.5) | collective-permute-done | bytes 262176 | tf_op jit(solution)/shard_map/image/ppermute | solution.py:639
  53.8 11.9 %all_to_all.10.parts = f32[16,32,128]{2,1,0:T(8,128)S(1)} all-to-all(f32[16,32,128]{2,1,0:T(8,128)S(1)} %fusion), channel_id=1, replica_groups={{0,1,64,65,4,5,68,69,8,9,72,73,12,13,76,77},{32,33,96,97,36,37,100,101,..., dimensions={0} | all-to-all | bytes 524288 | tf_op jit(solution)/shard_map/image/all_to_all | solution.py:640
  65.7 0.7 %image.1 = f32[1,32,128]{2,1,0:T(8,128)} custom-call(f32[16,32,128]{2,1,0:T(8,128)S(1)} %all_to_all.10.parts), custom_call_target="tpu_custom_call" | custom-call | tf_op jit(solution)/shard_map/image/pallas_call | solution.py:172
  (5 shorter events, 0.1 us)
Async XLA Ops:
  0.0 22.7 %copy-start = (f32[64,9,2,64]{3,2,1,0:T(2,128)S(1)}, f32[64,9,2,64]{3,2,1,0:T(2,128)}, u32[]{:S(2)}) copy-start(f32[64,9,2,64]{3,2,1,0:T(2,128)} %param.4) | copy-start | bytes 884740
  2.3 20.3 %all-to-all-start = ((f32[16,3,32,128]{3,2,1,0:T(8,128)}), f32[16,3,32,128]{3,2,1,0:T(8,128)S(1)}, u32[]{:S(2)}, u32[]{:S(2)}) async-start(f32[16,3,32,128]{3,2,1,0:T(8,128)} %pack.1), calls=%async_computation | async-start | bytes 1572864 | tf_op jit(solution)/shard_map/spread/all_to_all | solution.py:620
  22.6 6.3 %collective-permute-start = (f32[16,32,128]{2,1,0:T(8,128)S(1)}, f32[16,32,128]{2,1,0:T(8,128)S(1)}, u32[]{:S(2)}, u32[]{:S(2)}) collective-permute-start(f32[16,32,128]{2,1,0:T(8,128)S(1)} %slice_bitcast_fusion.2), channel_id=1, source_target_pairs={{0,32},{32,0},{64,96},{96,64},{4,36},{36,4},{68,100},{100,68},{1,3... | collective-permute-start | bytes 786440 | tf_op jit(solution)/shard_map/velocity/ppermute | solution.py:627
  23.0 11.9 %collective-permute-start.1 = (f32[10,32,128]{2,1,0:T(8,128)S(1)}, f32[10,32,128]{2,1,0:T(8,128)S(1)}, u32[]{:S(2)}, u32[]{:S(2)}) collective-permute-start(f32[10,32,128]{2,1,0:T(8,128)S(1)} %get-tuple-element.19), channel_id=1, source_target_pairs={{0,24},{32,56},{64,88},{96,120},{4,28},{36,60},{68,92},{100,124},{... | collective-permute-start | bytes 491528 | tf_op jit(solution)/shard_map/halo/ppermute | solution.py:623
  25.2 9.7 %collective-permute-start.2 = (f32[3,64,128]{2,1,0:T(8,128)S(1)}, f32[3,64,128]{2,1,0:T(8,128)S(1)}, u32[]{:S(2)}, u32[]{:S(2)}) collective-permute-start(f32[3,64,128]{2,1,0:T(8,128)S(1)} %get-tuple-element.20), channel_id=1, source_target_pairs={{0,3},{32,35},{64,67},{96,99},{4,7},{36,39},{68,71},{100,103},{1,2... | collective-permute-start | bytes 294920 | tf_op jit(solution)/shard_map/halo/ppermute | solution.py:624
  27.4 7.5 %collective-permute-start.3 = (f32[3,32,128]{2,1,0:T(8,128)S(1)}, f32[3,32,128]{2,1,0:T(8,128)S(1)}, u32[]{:S(2)}, u32[]{:S(2)}) collective-permute-start(f32[3,32,128]{2,1,0:T(8,128)S(1)} %get-tuple-element.21), channel_id=1, source_target_pairs={{0,27},{32,59},{64,91},{96,123},{4,31},{36,63},{68,95},{100,127},{... | collective-permute-start | bytes 147464 | tf_op jit(solution)/shard_map/halo/ppermute | solution.py:625
  34.9 1.4 %collective-permute-start.4 = (f32[5,32,128]{2,1,0:T(8,128)S(1)}, f32[5,32,128]{2,1,0:T(8,128)S(1)}, u32[]{:S(2)}, u32[]{:S(2)}) collective-permute-start(f32[5,32,128]{2,1,0:T(8,128)S(1)} %velocity.1), channel_id=1, source_target_pairs={{0,32},{32,0},{64,96},{96,64},{4,36},{36,4},{68,100},{100,68},{1,3... | collective-permute-start | bytes 245768 | tf_op jit(solution)/shard_map/velocity/ppermute | solution.py:631
  52.2 1.6 %collective-permute-start.5 = (f32[16,32,128]{2,1,0:T(8,128)S(1)}, f32[16,32,128]{2,1,0:T(8,128)S(1)}, u32[]{:S(2)}, u32[]{:S(2)}) collective-permute-start(f32[16,32,128]{2,1,0:T(8,128)S(1)} %slice_bitcast_fusion), channel_id=1, source_target_pairs={{0,32},{32,0},{64,96},{96,64},{4,36},{36,4},{68,100},{100,68},{1,3... | collective-permute-start | bytes 786440 | tf_op jit(solution)/shard_map/image/ppermute | solution.py:639
